TPU v7x, 128 devices: a whole 4x4x4 slice. The times are simulated.
128 devices in a mesh: fsdp: 16 (over y_hi, z, core), ctx: 2 (over y_lo), tp: 4 (over x).
Axes of the slice: x: 4, y: 4 (y_hi: 2, y_lo: 2; y = y_hi * 2 + y_lo), z: 4, core: 2. Of those that a mesh axis runs over, the one named last changes fastest.
Arguments:
- tokens: bfloat16 [32768, 1024], P(('fsdp', 'ctx')), may hold values from -6 to 6
- cotangent: bfloat16 [32768, 1024], P(('fsdp', 'ctx')), may hold values from -6 to 6
- expert_ids: int32 [32768, 1], P(('fsdp', 'ctx')), may hold values from 0 to 63
- segment_ids: int32 [32768], P('fsdp'), may hold values from 0 to 162, never falling along the last dimension, each value on 1 to 800 neighbouring positions
- priority: int32 [32, 1024], P(('fsdp', 'ctx')), may hold values from 0 to 1023, each once within a row
- w_qkv: bfloat16 [3, 1024, 1024], P(None, ('fsdp', 'ctx'), 'tp'), may hold values from -0.1875 to 0.1875
- w_out: bfloat16 [1024, 1024], P('tp', ('fsdp', 'ctx')), may hold values from -0.75 to 0.75
- norm_gains: bfloat16 [2, 1024], P(None, ('fsdp', 'ctx')), may hold values from 0.5 to 1.5
- norm_shifts: bfloat16 [3, 1024], P(None, ('fsdp', 'ctx')), may hold values from -0.59765625 to 0.59765625
- qv_bias: bfloat16 [2, 16, 64], P(None, 'tp', ('fsdp', 'ctx')), may hold values from -0.59765625 to 0.59765625
- w_up: bfloat16 [64, 1024, 4096], P(('fsdp', 'ctx'), None, 'tp'), may hold values from -0.1875 to 0.1875
- up_bias: bfloat16 [64, 4096], P(('fsdp', 'ctx'), 'tp'), may hold values from -0.59765625 to 0.59765625
- w_down: bfloat16 [64, 4096, 1024], P(('fsdp', 'ctx'), 'tp'), may hold values from -0.125 to 0.125
- down_bias: bfloat16 [64, 1024], P(('fsdp', 'ctx')), may hold values from -2.390625 to 2.390625
Outputs:
- block_out: bfloat16 [32768, 1024], P(('fsdp', 'ctx'))
- tokens_grad: bfloat16 [32768, 1024], P(('fsdp', 'ctx'))
- w_qkv_grad: float32 [3, 1024, 1024], P(None, ('fsdp', 'ctx'), 'tp')
- w_out_grad: float32 [1024, 1024], P('tp', ('fsdp', 'ctx'))
- norm_gains_grad: float32 [2, 1024], P(None, ('fsdp', 'ctx'))
- norm_shifts_grad: float32 [3, 1024], P(None, ('fsdp', 'ctx'))
- qv_bias_grad: float32 [2, 16, 64], P(None, 'tp', ('fsdp', 'ctx'))
- w_up_grad: float32 [64, 1024, 4096], P(('fsdp', 'ctx'), None, 'tp')
- up_bias_grad: float32 [64, 4096], P(('fsdp', 'ctx'), 'tp')
- w_down_grad: float32 [64, 4096, 1024], P(('fsdp', 'ctx'), 'tp')
- down_bias_grad: float32 [64, 1024], P(('fsdp', 'ctx'))
Inputs may be any that keep to these rules, and one draw needn't show every extreme that they name: `expert_ids`: every expert is named by some token. `segment_ids`: never falls along the array; one id covers 1 to 800 consecutive positions, some id exactly 800. `priority`: each row is a permutation of the positions of its block.
All inputs are finite; a program needn't handle non-finite values.
Results may differ from a plain program's by a relative error of at most 0.03.
Values may be sent and summed in bfloat16 or wider, within the bound.
No kernel may reach another device: no remote copies, remote signals or barrier semaphores. Data moves between devices by JAX's collectives and lax.ppermute only.
A program may use at most 192 MiB of HBM per device.

v0:
```python
import jax
import jax.numpy as jnp
from jax import lax
from jax.sharding import PartitionSpec as P

HD = 64


EPSILON = 1e-05
NEGATIVE = -1e30


def in_one_piece(arrays, axis, dim, along):
    both = jnp.concatenate(arrays, axis=along)
    whole, at, gathered = (lax.all_gather(both, axis, axis=dim, tiled=True), 0, [])
    for a in arrays:
        gathered.append(lax.slice_in_dim(whole, at, at + a.shape[along], axis=along))
        at += a.shape[along]
    return tuple(gathered)


def copy_for_each(shard, axis):
    peers = lax.axis_size(axis)
    return lax.all_to_all(
        jnp.broadcast_to(shard[None], (peers, *shard.shape)), axis, 0, 0, tiled=True
    )


def joined_along(tiles, dim):
    lengths = list(tiles.shape[1:])
    lengths[dim] *= tiles.shape[0]
    return jnp.moveaxis(tiles, 0, dim).reshape(lengths)


def gather_directly(shard, axis, dim):
    tiles = copy_for_each(shard, axis)
    return joined_along(tiles, dim)


def sent_together(arrays, axis, dim, along):
    both = jnp.concatenate(arrays, axis=along)
    whole, at, gathered = (gather_directly(both, axis, dim), 0, [])
    for a in arrays:
        gathered.append(lax.slice_in_dim(whole, at, at + a.shape[along], axis=along))
        at += a.shape[along]
    return tuple(gathered)


def joined_by_halves(pieces, combine):
    while len(jax.tree.leaves(pieces)[0]) > 1:
        pieces = jax.vmap(combine)(*(pieces[side::2] for side in (0, 1)))
    return pieces[0]


def prefix(shard, axis, combine, identity):
    peers, mine = (lax.axis_size(axis), lax.axis_index(axis))
    passed = jnp.arange(peers) < mine

    def kept(part, zero, own):
        part = jnp.where(
            passed.reshape(-1, *(1 for _ in own.shape)), part, jnp.asarray(zero, own.dtype)
        )
        return part

    pieces = copy_for_each(shard, axis)
    return joined_by_halves(kept(pieces, identity, shard), combine)


def in_one_piece_2(arrays, axis, split_dim, concat_dim, along):
    widths = [a.shape[along] for a in arrays]
    both = jnp.concatenate(arrays, axis=along)
    whole = lax.all_to_all(both, axis, split_axis=split_dim, concat_axis=concat_dim, tiled=True)
    return tuple(jnp.split(whole, [sum(widths[:k]) for k in range(1, len(widths))], axis=along))


def in_one_piece_3(arrays, axis, dim, along):
    widths = [a.shape[along] for a in arrays]
    both = jnp.concatenate(arrays, axis=along)
    whole = lax.psum_scatter(both, axis, scatter_dimension=dim, tiled=True)
    return tuple(jnp.split(whole, [sum(widths[:k]) for k in range(1, len(widths))], axis=along))


def in_blocks(shard, dim, peers):
    before, after = (shard.shape[:dim], shard.shape[dim + 1 :])
    return jnp.moveaxis(shard.reshape(*before, peers, -1, *after), dim, 0)


def summed_on_arrival(shard, axis, dim):
    tiles = in_blocks(shard, dim, lax.axis_size(axis))
    arrived = lax.all_to_all(tiles, axis, split_axis=0, concat_axis=0, tiled=True)
    return arrived.astype(jnp.float32).sum(axis=0)


def side_by_side(arrays, axis, dim, along):
    widths = [a.shape[along] for a in arrays]
    both = jnp.concatenate(arrays, axis=along)
    whole = summed_on_arrival(both, axis, dim)
    return tuple(jnp.split(whole, [sum(widths[:k]) for k in range(1, len(widths))], axis=along))


def norm_forward(values, gain_row, shift_row):
    centre = values - jnp.mean(values, axis=-1, keepdims=True)
    variance = jnp.mean(centre * centre, axis=-1, keepdims=True)
    inverse = lax.rsqrt(variance + EPSILON)
    normed = centre * inverse
    return (normed * gain_row + shift_row, normed, inverse)


def norm_backward(grad_out, normed, inverse, gain_row):
    scaled = grad_out * gain_row
    inner = jnp.mean(scaled, axis=-1, keepdims=True)
    along = jnp.mean(scaled * normed, axis=-1, keepdims=True)
    return inverse * (scaled - inner - normed * along)


def allowed_pairs(seg_query, pos_query, seg_keys, pos_keys):
    return (seg_query[:, None] == seg_keys[None, :]) & (pos_keys[None, :] <= pos_query[:, None])


def add_counts(earlier, later):
    return earlier + later


def attend_forward(
    query_blocks, seg_blocks, pos_blocks, key_all, value_all, seg_keys, pos_keys, factor
):

    def one_block(block_parts):
        query_blk, seg_blk, pos_blk = block_parts
        scores = (
            jnp.einsum("qhd,khd->hqk", query_blk, key_all, preferred_element_type=jnp.float32)
            * factor
        )
        allowed = allowed_pairs(seg_blk, pos_blk, seg_keys, pos_keys)[None]
        scores = jnp.where(allowed, scores, NEGATIVE)
        row_peak = jnp.max(scores, axis=-1, keepdims=True)
        row_total = jnp.sum(jnp.exp(scores - row_peak), axis=-1, keepdims=True)
        log_total = row_peak + jnp.log(row_total)
        weights = jnp.exp(scores - log_total)
        weights_low = weights.astype(jnp.bfloat16)
        weights_rest = (weights - weights_low.astype(jnp.float32)).astype(jnp.bfloat16)
        mixed_part = jnp.einsum(
            "hqk,khd->qhd", weights_low, value_all, preferred_element_type=jnp.float32
        )
        extra_part = jnp.einsum(
            "hqk,khd->qhd", weights_rest, value_all, preferred_element_type=jnp.float32
        )
        return (mixed_part, mixed_part + extra_part, log_total[..., 0])

    return lax.map(one_block, (query_blocks, seg_blocks, pos_blocks))


def attend_backward(
    query_blocks,
    grad_blocks,
    exact_blocks,
    lse_blocks,
    seg_blocks,
    pos_blocks,
    key_all,
    value_all,
    seg_keys,
    pos_keys,
    factor,
):
    key_zero = jnp.zeros(key_all.shape, jnp.float32)

    def one_block(running_grads, block_parts):
        key_grad, value_grad = running_grads
        query_blk, grad_blk, exact_blk, lse_blk, seg_blk, pos_blk = block_parts
        scores = (
            jnp.einsum("qhd,khd->hqk", query_blk, key_all, preferred_element_type=jnp.float32)
            * factor
        )
        allowed = allowed_pairs(seg_blk, pos_blk, seg_keys, pos_keys)[None]
        scores = jnp.where(allowed, scores, NEGATIVE)
        weights = jnp.exp(scores - lse_blk[..., None])
        weights_low = weights.astype(jnp.bfloat16)
        grad_weights = jnp.einsum(
            "qhd,khd->hqk", grad_blk, value_all, preferred_element_type=jnp.float32
        )
        center = jnp.einsum("qhd,qhd->hq", grad_blk.astype(jnp.float32), exact_blk)
        grad_scores = (weights * (grad_weights - center[..., None])).astype(jnp.bfloat16)
        query_grad = (
            jnp.einsum("hqk,khd->qhd", grad_scores, key_all, preferred_element_type=jnp.float32)
            * factor
        )
        key_grad = (
            key_grad
            + jnp.einsum("hqk,qhd->khd", grad_scores, query_blk, preferred_element_type=jnp.float32)
            * factor
        )
        value_grad = value_grad + jnp.einsum(
            "hqk,qhd->khd", weights_low, grad_blk, preferred_element_type=jnp.float32
        )
        return ((key_grad, value_grad), query_grad)

    (key_grad, value_grad), query_grads = lax.scan(
        one_block,
        (key_zero, key_zero),
        (query_blocks, grad_blocks, exact_blocks, lse_blocks, seg_blocks, pos_blocks),
    )
    return (key_grad, value_grad, query_grads)


def join_context(received, per_device, fsdp_count, ctx_count, capacity, send_width):
    shaped = received.reshape(per_device, fsdp_count, ctx_count, capacity, send_width)
    joined = shaped[:, :, 0]
    joined = joined + shaped[:, :, 1]
    return joined.reshape(per_device, fsdp_count * capacity, send_width)


def on_device(
    tokens,
    cotangent,
    expert_ids,
    segment_ids,
    priority,
    w_qkv,
    w_out,
    norm_gains,
    norm_shifts,
    qv_bias,
    w_up,
    up_bias,
    w_down,
    down_bias,
):
    qkv_full, out_full, gains_full, shifts_full, bias_full = (
        lax.all_gather(w_qkv, ("fsdp", "ctx"), axis=1, tiled=True),
        *in_one_piece((w_out, norm_gains, norm_shifts), ("fsdp", "ctx"), 1, 0),
        lax.all_gather(qv_bias, ("fsdp", "ctx"), axis=2, tiled=True),
    )
    gain_rows = gains_full.astype(jnp.float32)
    shift_rows = shifts_full.astype(jnp.float32)
    row_count, model_width = tokens.shape
    channels = qkv_full.shape[2]
    heads_here = channels // HD
    factor = HD ** (-0.5)
    seq_len = segment_ids.shape[0]
    fsdp_count = lax.axis_size("fsdp")
    ctx_count = lax.axis_size("ctx")
    tp_count = lax.axis_size("tp")
    per_device = w_up.shape[0]
    expert_count = per_device * fsdp_count * ctx_count
    capacity = (9 * seq_len + 8 * expert_count - 1) // (8 * expert_count)
    inputs = tokens.astype(jnp.float32)
    first_norm, normed_one, inverse_one = norm_forward(inputs, gain_rows[0], shift_rows[0])
    first_low = first_norm.astype(jnp.bfloat16)
    projected = jnp.einsum("rd,tdc->trc", first_low, qkv_full, preferred_element_type=jnp.float32)
    bias_flat = bias_full.astype(jnp.float32).reshape(2, channels)
    query_low = (projected[0] + bias_flat[0]).astype(jnp.bfloat16)
    key_low = projected[1].astype(jnp.bfloat16)
    value_low = (projected[2] + bias_flat[1]).astype(jnp.bfloat16)
    key_all, value_all = sent_together((key_low, value_low), "ctx", 0, 1)
    key_all = key_all.reshape(seq_len, heads_here, HD)
    value_all = value_all.reshape(seq_len, heads_here, HD)
    block_rows = min(512, row_count)
    block_count = row_count // block_rows
    ctx_at = lax.axis_index("ctx")
    pos_local = ctx_at * row_count + jnp.arange(row_count, dtype=jnp.int32)
    seg_local = lax.dynamic_slice_in_dim(segment_ids, ctx_at * row_count, row_count)
    pos_keys = jnp.arange(seq_len, dtype=jnp.int32)
    query_blocks = query_low.reshape(block_count, block_rows, heads_here, HD)
    seg_blocks = seg_local.reshape(block_count, block_rows)
    pos_blocks = pos_local.reshape(block_count, block_rows)
    mixed_out, exact_out, log_totals = attend_forward(
        query_blocks, seg_blocks, pos_blocks, key_all, value_all, segment_ids, pos_keys, factor
    )
    mixed_low = mixed_out.reshape(row_count, channels).astype(jnp.bfloat16)
    branch_part = jnp.dot(mixed_low, out_full, preferred_element_type=jnp.float32)
    branch = lax.psum(branch_part, "tp") + shift_rows[2]
    middle = inputs + branch
    second, normed_two, inverse_two = norm_forward(middle, gain_rows[1], shift_rows[1])
    second_low = second.astype(jnp.bfloat16)
    owner_ids = expert_ids[:, 0]
    rank_list = priority[0]
    expert_range = jnp.arange(expert_count, dtype=jnp.int32)
    in_order = jnp.zeros((row_count,), jnp.int32).at[rank_list].set(owner_ids)
    order_table = (in_order[:, None] == expert_range[None, :]).astype(jnp.int32)
    running = jnp.cumsum(order_table, axis=0)
    rank_sorted = jnp.sum(running * order_table, axis=1) - 1
    local_slot = rank_sorted[rank_list]
    counts = running[-1]
    carried = prefix(counts, "ctx", add_counts, jnp.zeros_like(counts))
    owner_table = (owner_ids[:, None] == expert_range[None, :]).astype(jnp.int32)
    slot_index = jnp.sum(owner_table * carried[None, :], axis=1) + local_slot
    dead_row = expert_count * capacity
    target = jnp.where(slot_index < capacity, owner_ids * capacity + slot_index, dead_row).astype(
        jnp.int32
    )
    token_at = (
        jnp.full((dead_row,), row_count, jnp.int32)
        .at[target]
        .set(jnp.arange(row_count, dtype=jnp.int32), mode="drop")
    )
    zero_row = jnp.zeros((1, model_width), jnp.bfloat16)
    send_rows = jnp.concatenate([second_low, zero_row], axis=0)[token_at]
    send_grads = jnp.concatenate([cotangent, zero_row], axis=0)[token_at]
    send_width = model_width // tp_count
    column_start = lax.axis_index("tp") * send_width
    send_rows = lax.dynamic_slice_in_dim(send_rows, column_start, send_width, 1)
    send_grads = lax.dynamic_slice_in_dim(send_grads, column_start, send_width, 1)
    bias_columns = lax.dynamic_slice_in_dim(down_bias, column_start, send_width, 1)
    send_shape = (fsdp_count * ctx_count, per_device, capacity, send_width)
    got_rows, got_grads = in_one_piece_2(
        (send_rows.reshape(send_shape), send_grads.reshape(send_shape)), ("fsdp", "ctx"), 0, 2, 1
    )
    expert_rows = join_context(got_rows, per_device, fsdp_count, ctx_count, capacity, send_width)
    expert_grads = join_context(got_grads, per_device, fsdp_count, ctx_count, capacity, send_width)
    expert_rows, expert_grads = in_one_piece((expert_rows, expert_grads), "tp", 2, 0)
    hidden = (
        jnp.einsum("emd,edf->emf", expert_rows, w_up, preferred_element_type=jnp.float32)
        + up_bias.astype(jnp.float32)[:, None, :]
    )
    sigmoid_hidden = jax.nn.sigmoid(hidden)
    active_low = (hidden * sigmoid_hidden).astype(jnp.bfloat16)
    slope = sigmoid_hidden * (1.0 + hidden * (1.0 - sigmoid_hidden))
    result_part = jnp.einsum("emf,efd->emd", active_low, w_down, preferred_element_type=jnp.float32)
    active_grad = jnp.einsum(
        "emd,efd->emf", expert_grads, w_down, preferred_element_type=jnp.float32
    )
    hidden_grad = (active_grad * slope).astype(jnp.bfloat16)
    input_part = jnp.einsum("emf,edf->emd", hidden_grad, w_up, preferred_element_type=jnp.float32)
    w_up_grad = jnp.einsum(
        "emd,emf->edf", expert_rows, hidden_grad, preferred_element_type=jnp.float32
    )
    w_down_grad = jnp.einsum(
        "emf,emd->efd", active_low, expert_grads, preferred_element_type=jnp.float32
    )
    up_bias_grad = jnp.sum(hidden_grad.astype(jnp.float32), axis=1)
    down_bias_grad = jnp.sum(expert_grads.astype(jnp.float32), axis=1)
    result_sum, input_sum = tuple(
        (
            part.astype(jnp.float32)
            for part in in_one_piece_3(
                (result_part.astype(jnp.bfloat16), input_part.astype(jnp.bfloat16)), "tp", 2, 0
            )
        )
    )
    result_low = (result_sum + bias_columns.astype(jnp.float32)[:, None, :]).astype(jnp.bfloat16)
    input_low = input_sum.astype(jnp.bfloat16)
    spread_shape = (per_device, fsdp_count, 1, capacity, send_width)
    full_shape = (per_device, fsdp_count, ctx_count, capacity, send_width)
    flat_shape = (1, per_device, fsdp_count * ctx_count * capacity, send_width)
    back_rows, back_grads = in_one_piece_2(
        (
            jnp.broadcast_to(result_low.reshape(spread_shape), full_shape).reshape(flat_shape),
            jnp.broadcast_to(input_low.reshape(spread_shape), full_shape).reshape(flat_shape),
        ),
        ("fsdp", "ctx"),
        2,
        0,
        1,
    )
    back_rows = back_rows.reshape(dead_row, send_width)
    back_grads = back_grads.reshape(dead_row, send_width)
    back_rows, back_grads = in_one_piece((back_rows, back_grads), "tp", 1, 0)
    expert_out = jnp.concatenate([back_rows, zero_row], axis=0)[target]
    second_grad = jnp.concatenate([back_grads, zero_row], axis=0)[target].astype(jnp.float32)
    block_out = (middle + expert_out.astype(jnp.float32)).astype(jnp.bfloat16)
    middle_grad = cotangent.astype(jnp.float32) + norm_backward(
        second_grad, normed_two, inverse_two, gain_rows[1]
    )
    gain_two = jnp.sum(second_grad * normed_two, axis=0)
    shift_two = jnp.sum(second_grad, axis=0)
    branch_low = middle_grad.astype(jnp.bfloat16)
    shift_out = jnp.sum(branch_low.astype(jnp.float32), axis=0)
    w_out_grad = jnp.einsum("rc,rd->cd", mixed_low, branch_low, preferred_element_type=jnp.float32)
    mixed_grad = jnp.einsum(
        "rd,cd->rc", branch_low, out_full, preferred_element_type=jnp.float32
    ).astype(jnp.bfloat16)
    grad_blocks = mixed_grad.reshape(block_count, block_rows, heads_here, HD)
    key_grad, value_grad, query_grads = attend_backward(
        query_blocks,
        grad_blocks,
        exact_out,
        log_totals,
        seg_blocks,
        pos_blocks,
        key_all,
        value_all,
        segment_ids,
        pos_keys,
        factor,
    )
    key_own, value_own = side_by_side(
        (key_grad.astype(jnp.bfloat16), value_grad.astype(jnp.bfloat16)), "ctx", 0, 1
    )
    query_low_grad = query_grads.reshape(row_count, channels).astype(jnp.bfloat16)
    value_low_grad = value_own.reshape(row_count, channels).astype(jnp.bfloat16)
    stacked = jnp.stack(
        [query_low_grad, key_own.reshape(row_count, channels).astype(jnp.bfloat16), value_low_grad]
    )
    w_qkv_grad = jnp.einsum("rd,trc->tdc", first_low, stacked, preferred_element_type=jnp.float32)
    first_part = jnp.einsum("trc,tdc->rd", stacked, qkv_full, preferred_element_type=jnp.float32)
    first_grad = lax.psum(first_part.astype(jnp.bfloat16), "tp").astype(jnp.float32)
    tokens_grad = (
        middle_grad + norm_backward(first_grad, normed_one, inverse_one, gain_rows[0])
    ).astype(jnp.bfloat16)
    gain_one = jnp.sum(first_grad * normed_one, axis=0)
    shift_one = jnp.sum(first_grad, axis=0)
    bias_grad = jnp.stack(
        [
            jnp.sum(query_low_grad.astype(jnp.float32), axis=0),
            jnp.sum(value_low_grad.astype(jnp.float32), axis=0),
        ]
    ).reshape(2, heads_here, HD)
    gain_grad = jnp.stack([gain_one, gain_two])
    shift_grad = jnp.stack([shift_one, shift_two, shift_out])
    qkv_shard, out_shard, gain_shard, shift_shard, bias_shard = (
        lax.psum_scatter(
            w_qkv_grad.astype(jnp.bfloat16), ("fsdp", "ctx"), scatter_dimension=1, tiled=True
        ).astype(jnp.float32),
        *tuple(
            (
                part.astype(jnp.float32)
                for part in in_one_piece_3(
                    (
                        w_out_grad.astype(jnp.bfloat16),
                        gain_grad.astype(jnp.bfloat16),
                        shift_grad.astype(jnp.bfloat16),
                    ),
                    ("fsdp", "ctx"),
                    1,
                    0,
                )
            )
        ),
        lax.psum_scatter(
            bias_grad.astype(jnp.bfloat16), ("fsdp", "ctx"), scatter_dimension=2, tiled=True
        ).astype(jnp.float32),
    )
    return (
        block_out,
        tokens_grad,
        qkv_shard,
        out_shard,
        gain_shard,
        shift_shard,
        bias_shard,
        w_up_grad,
        up_bias_grad,
        w_down_grad,
        down_bias_grad,
    )


def solution(mesh):
    return jax.shard_map(
        on_device,
        mesh=mesh,
        in_specs=(
            P(("fsdp", "ctx"), None),
            P(("fsdp", "ctx"), None),
            P(("fsdp", "ctx"), None),
            P("fsdp"),
            P(("fsdp", "ctx"), None),
            P(None, ("fsdp", "ctx"), "tp"),
            P("tp", ("fsdp", "ctx")),
            P(None, ("fsdp", "ctx")),
            P(None, ("fsdp", "ctx")),
            P(None, "tp", ("fsdp", "ctx")),
            P(("fsdp", "ctx"), None, "tp"),
            P(("fsdp", "ctx"), "tp"),
            P(("fsdp", "ctx"), "tp", None),
            P(("fsdp", "ctx"), None),
        ),
        out_specs=(
            P(("fsdp", "ctx"), None),
            P(("fsdp", "ctx"), None),
            P(None, ("fsdp", "ctx"), "tp"),
            P("tp", ("fsdp", "ctx")),
            P(None, ("fsdp", "ctx")),
            P(None, ("fsdp", "ctx")),
            P(None, "tp", ("fsdp", "ctx")),
            P(("fsdp", "ctx"), None, "tp"),
            P(("fsdp", "ctx"), "tp"),
            P(("fsdp", "ctx"), "tp", None),
            P(("fsdp", "ctx"), None),
        ),
        check_vma=False,
    )
```

profile of v0, /device:TPU:0, one launch (start us, length us, event | category | flops | bytes accessed | tf_op | source)
XLA Modules:
  0.0 1153.6 jit_solution(15270499613596276024)
XLA Ops:
  10.1 67.1 %all_gather.17 = bf16[2,4,64]{1,0,2:T(2,128)(2,1)S(1)} all-gather(bf16[2,4,2]{1,0,2:T(2,128)(2,1)S(1)} %copy.130), channel_id=1, replica_groups=mesh['fsdp'=16,'ctx'=2,'tp'=4] {'fsdp','ctx'}, dimensions={2}, use_global_device_ids=true | all-gather | bytes 1056 | tf_op jit(solution)/shard_map/all_gather | solution.py:232
  78.3 65.3 %all_gather.15 = bf16[261,1024]{0,1:T(8,128)(2,1)S(1)} all-gather(bf16[261,32]{0,1:T(8,128)(2,1)S(1)} %pad_maximum_fusion.9), channel_id=1, replica_groups=mesh['fsdp'=16,'ctx'=2,'tp'=4] {'fsdp','ctx'}, dimensions={1}, use_global_device_ids=true | all-gather | bytes 551232 | tf_op jit(solution)/shard_map/all_gather | solution.py:15
  160.5 21.6 %all-to-all-done = bf16[2,1024,512]{1,2,0:T(8,128)(2,1)} async-done(((bf16[2,1024,512]{1,2,0:T(8,128)(2,1)}), bf16[2,1024,512]{1,2,0:T(8,128)(2,1)}, u32[]{:S(2)}, u32[]{:S(2)}) %all-to-all-start) | async-done | bytes 2097184 | tf_op jit(solution)/shard_map/all_to_all | solution.py:24
  191.9 38.2 %while.32 = (s32[]{:T(128)}, bf16[2,512,4,64]{1,3,2,0:T(8,128)(2,1)S(1)}, f32[2,512,4,64]{1,3,2,0:T(8,128)}, f32[2,4,512]{2,1,0:T(4,128)S(1)}, s32[2,512]{1,0:T(...) while((s32[]{:T(128)}, ...), condition=%wide.region_5.6_spmd.clone.clone, body=%wide.region_2.5_spmd.clone.sunk.clone | while | flops 1689384960 | bytes 90534096 | solution.py:150
  238.0 18.0 %reduce-window.6 = s32[64,8,128]{2,1,0:T(8,128)S(1)} reduce-window(s32[64,8,128]{2,1,0:T(8,128)S(1)} %fusion.95, s32[]{:T(128)} %copy.231), window={size=1x1x128 pad=0_0x0_0x127_0}, to_apply=%region_10.11 | reduce-window | flops 8323072 | bytes 524292 | tf_op jit(solution)/shard_map/reduce-window
  272.8 8.1 gather_fusion.2
  280.9 43.3 %all-reduce.9.cloned.1.call-done = f32[1024,1024]{1,0:T(8,128)} async-done(((f32[1024,1024]{1,0:T(8,128)}), f32[1024,1024]{1,0:T(8,128)}) %all-reduce.9.cloned.1.call-update) | async-done | bytes 4194320 | tf_op jit(solution)/shard_map/psum | solution.py:272
  330.0 8.1 gather_fusion.1
  346.7 39.2 %all_to_all.55 = bf16[32,4,36,256]{3,1,2,0:T(4,128)(2,1)S(1)} all-to-all(bf16[32,4,36,256]{3,1,2,0:T(4,128)(2,1)S(1)} %copy.141), channel_id=1, replica_groups=mesh['fsdp'=16,'ctx'=2,'tp'=4] {'fsdp','ctx'}, dimensions={0} | all-to-all | bytes 4718592 | tf_op jit(solution)/shard_map/all_to_all | solution.py:72
  390.2 52.3 %all-gather.6.cloned.1.call-done = bf16[4,576,1024]{2,1,0:T(8,128)(2,1)} async-done(((bf16[4,576,256]{2,1,0:T(8,128)(2,1)}), bf16[4,576,1024]{2,1,0:T(8,128)(2,1)}) %all-gather.6.cloned.1.call-update) | async-done | bytes 4718608 | tf_op jit(solution)/shard_map/all_gather | solution.py:15
  463.3 51.3 %reduce-scatter.6.cloned.1.call-done = bf16[4,576,256]{2,1,0:T(8,128)(2,1)} async-done(((bf16[4,576,1024]{2,1,0:T(8,128)(2,1)}), bf16[4,576,256]{2,1,0:T(8,128)(2,1)}) %reduce-scatter.6.cloned.1.call-update) | async-done | bytes 1179664 | tf_op jit(solution)/shard_map/reduce_scatter | solution.py:79
  522.3 39.0 %all_to_all.56 = bf16[1,4,1152,256]{3,1,0,2:T(4,128)(2,1)S(1)} all-to-all(bf16[1,4,1152,256]{3,1,0,2:T(4,128)(2,1)S(1)} %maximum_bitcast_fusion), channel_id=1, replica_groups=mesh['fsdp'=16,'ctx'=2,'tp'=4] {'fsdp','ctx'}, dimensions={2} | all-to-all | bytes 4718592 | tf_op jit(solution)/shard_map/all_to_all | solution.py:72
  567.7 91.9 %all-gather.8.cloned.1.call-done = bf16[4608,1024]{1,0:T(8,128)(2,1)} async-done(((bf16[4608,256]{1,0:T(8,128)(2,1)}), bf16[4608,1024]{1,0:T(8,128)(2,1)}) %all-gather.8.cloned.1.call-update) | async-done | bytes 9437200 | tf_op jit(solution)/shard_map/all_gather | solution.py:15
  677.1 9.0 gather_fusion.3
  699.4 98.5 %while.33 = (s32[]{:T(128)}, f32[2048,4,64]{0,2,1:T(8,128)}, f32[2048,4,64]{0,2,1:T(8,128)}, bf16[2,512,4,64]{1,3,2,0:T(8,128)(2,1)}, bf16[2,512,4,64]{1,3,2,0:T...) while((s32[]{:T(128)}, f32[2048,4,64]{0,2,1:T(8,128)}, ...), condition=%wide.region_19.20_spmd.clone.clone, body=%wide.region_18.19_spmd.clone.sunk.clone | while | flops 2732587008 | bytes 206002608 | solution.py:198
  716.9 9.9 multiply_convert_fusion.7
  736.1 11.9 %fusion.199 = f32[2048,4,64]{0,2,1:T(8,128)} fusion(f32[4,512,2048]{2,1,0:T(8,128)} %copy-done.1, f32[4,512]{1,0:T(4,128)S(1)} %copy-done.32, pred[512,2048]{1,0:T(8,128)(4,1)S(1)} %copy-done.8, f32[2048,4,64]{0,2,1:T(8,128)} %get-tuple-element.704, pred[]{:T(512)S(6)} %compare.7, bf16[2,512,4,64]{1,3,2,0:T(8,128)(2,1)} %get-tuple-element.725, ...), kind=kOutput, calls=%fused_computation.52.clone.1.clone | convolution fusion | flops 554696704 | bytes 22290944 | tf_op jit(solution)/shard_map/while/body/eval_jaxpr/hqk,qhd->khd/dot_general | solution.py:193
  765.4 9.9 multiply_convert_fusion.7
  785.2 12.5 %fusion.199 = f32[2048,4,64]{0,2,1:T(8,128)} fusion(f32[4,512,2048]{2,1,0:T(8,128)} %copy-done.1, f32[4,512]{1,0:T(4,128)S(1)} %copy-done.32, pred[512,2048]{1,0:T(8,128)(4,1)S(1)} %copy-done.8, f32[2048,4,64]{0,2,1:T(8,128)} %get-tuple-element.704, pred[]{:T(512)S(6)} %compare.7, bf16[2,512,4,64]{1,3,2,0:T(8,128)(2,1)} %get-tuple-element.725, ...), kind=kOutput, calls=%fused_computation.52.clone.1.clone | convolution fusion | flops 554696704 | bytes 22290944 | tf_op jit(solution)/shard_map/while/body/eval_jaxpr/hqk,qhd->khd/dot_general | solution.py:193
  813.0 18.0 %all-to-all-done.4 = bf16[2,1024,8,64]{1,3,2,0:T(8,128)(2,1)S(1)} async-done(((bf16[2,1024,8,64]{1,3,2,0:T(8,128)(2,1)}), bf16[2,1024,8,64]{1,3,2,0:T(8,128)(2,1)S(1)}, u32[]{:S(2)}, u32[]{:S(2)}) %all-to-all-start.4) | async-done | bytes 2097184 | tf_op jit(solution)/shard_map/all_to_all | solution.py:90
  837.4 10.2 fusion.83
  850.3 8.7 fusion.113
  870.8 126.4 %all-reduce.4 = bf16[2,4,64]{1,2,0:T(8,128)(2,1)S(1)} all-reduce(bf16[2,4,64]{1,2,0:T(8,128)(2,1)S(1)} %copy.159), channel_id=5, replica_groups=mesh['fsdp'=16,'ctx'=2,'tp'=4] {'fsdp','ctx'}, use_global_device_ids=true, to_apply=%region_33.34.clone | all-reduce | flops 512 | bytes 2048
  1013.4 128.5 %reduce-scatter.8.cloned.1.call-done = bf16[32,261]{1,0:T(8,128)(2,1)} async-done(((bf16[1024,261]{1,0:T(8,128)(2,1)}), bf16[32,261]{1,0:T(8,128)(2,1)}) %reduce-scatter.8.cloned.1.call-update) | async-done | bytes 16720
  (384 shorter events, 285.1 us)
Async XLA Ops:
  7.2 138.8 %copy-start.5 = (bf16[1024,1024]{1,0:T(8,128)(2,1)S(1)}, bf16[1024,1024]{1,0:T(8,128)(2,1)}, u32[]{:S(2)}) copy-start(bf16[1024,1024]{1,0:T(8,128)(2,1)} %param.18) | copy-start | bytes 6291460
  7.2 139.8 %all-gather.4.cloned.1.call-start = ((), (), s32[]{:S(2)}) async-start(), calls=%async_computation.7 | async-start | bytes 1622016 | tf_op jit(solution)/shard_map/all_gather | solution.py:230
  154.2 28.0 %all-to-all-start = ((bf16[2,1024,512]{1,2,0:T(8,128)(2,1)}), bf16[2,1024,512]{1,2,0:T(8,128)(2,1)}, u32[]{:S(2)}, u32[]{:S(2)}) async-start(bf16[2,1024,512]{1,2,0:T(8,128)(2,1)} %broadcast_in_dim.76), calls=%async_computation | async-start | bytes 4194304 | tf_op jit(solution)/shard_map/all_to_all | solution.py:24
  159.1 165.1 %all-reduce.9.cloned.1.call-start = ((), (), s32[]{:S(2)}) async-start(), calls=%async_computation.8 | async-start | bytes 8388608 | tf_op jit(solution)/shard_map/psum | solution.py:272
  159.3 26.9 %copy-start.9 = (bf16[2,512,4,64]{1,3,2,0:T(8,128)(2,1)}, bf16[2,512,4,64]{1,3,2,0:T(8,128)(2,1)S(1)}, u32[]{:S(2)}) copy-start(bf16[2,512,4,64]{1,3,2,0:T(8,128)(2,1)S(1)} %fusion.110) | copy-start | bytes 1572868
  191.9 38.9 %copy-start.16 = (bf16[261,1024]{0,1:T(8,128)(2,1)S(1)}, bf16[261,1024]{0,1:T(8,128)(2,1)}, u32[]{:S(2)}) copy-start(bf16[261,1024]{0,1:T(8,128)(2,1)} %copy-done.15) | copy-start | bytes 1603588
  257.4 10.0 all-to-all-start.1
  260.6 181.9 %all-gather.6.cloned.1.call-start = ((), (), s32[]{:S(2)}) async-start(), calls=%async_computation.9 | async-start | bytes 5898240 | tf_op jit(solution)/shard_map/all_gather | solution.py:15
  272.8 51.4 %copy-start.50 = (f32[1024]{0:T(1024)S(1)}, f32[1024]{0:T(1024)}, u32[]{:S(2)}) copy-start(f32[1024]{0:T(1024)} %get-tuple-element.355) | copy-start | bytes 12292
  390.1 124.5 %reduce-scatter.6.cloned.1.call-start = ((), (), s32[]{:S(2)}) async-start(), calls=%async_computation.10 | async-start | bytes 5898240 | tf_op jit(solution)/shard_map/reduce_scatter | solution.py:79
  390.2 61.0 %copy-start.53 = (f32[2,1024]{1,0:T(2,128)}, f32[2,1024]{1,0:T(2,128)S(1)}, u32[]{:S(2)}) copy-start(f32[2,1024]{1,0:T(2,128)S(1)} %convert_element_type.214) | copy-start | bytes 24580
  462.6 197.0 %all-gather.8.cloned.1.call-start = ((), (), s32[]{:S(2)}) async-start(), calls=%async_computation.11 | async-start | bytes 11796480 | tf_op jit(solution)/shard_map/all_gather | solution.py:15
  677.1 9.0 copy-start.38
  677.1 9.0 copy-start.40
  677.1 9.0 copy-start.44
  736.1 11.9 %copy-start.11 = (bf16[2,512,4,64]{1,3,2,0:T(8,128)(2,1)}, bf16[2,512,4,64]{1,3,2,0:T(8,128)(2,1)S(1)}, u32[]{:S(2)}) copy-start(bf16[2,512,4,64]{1,3,2,0:T(8,128)(2,1)S(1)} %fusion.200) | copy-start | bytes 1572868 | tf_op jit(solution)/shard_map/while
  736.1 11.9 %copy-start.34 = (s32[2,512]{1,0:T(2,128)S(1)}, s32[2,512]{1,0:T(2,128)}, u32[]{:S(2)}) copy-start(s32[2,512]{1,0:T(2,128)} %copy-done.33) | copy-start | bytes 12292 | tf_op jit(solution)/shard_map/while
  785.2 12.5 %copy-start.11 = (bf16[2,512,4,64]{1,3,2,0:T(8,128)(2,1)}, bf16[2,512,4,64]{1,3,2,0:T(8,128)(2,1)S(1)}, u32[]{:S(2)}) copy-start(bf16[2,512,4,64]{1,3,2,0:T(8,128)(2,1)S(1)} %fusion.200) | copy-start | bytes 1572868 | tf_op jit(solution)/shard_map/while
  785.2 12.5 %copy-start.34 = (s32[2,512]{1,0:T(2,128)S(1)}, s32[2,512]{1,0:T(2,128)}, u32[]{:S(2)}) copy-start(s32[2,512]{1,0:T(2,128)} %copy-done.33) | copy-start | bytes 12292 | tf_op jit(solution)/shard_map/while
  803.1 27.9 %all-to-all-start.4 = ((bf16[2,1024,8,64]{1,3,2,0:T(8,128)(2,1)}), bf16[2,1024,8,64]{1,3,2,0:T(8,128)(2,1)S(1)}, u32[]{:S(2)}, u32[]{:S(2)}) async-start(bf16[2,1024,8,64]{1,3,2,0:T(8,128)(2,1)} %bitcast.251), calls=%async_computation.5 | async-start | bytes 4194304 | tf_op jit(solution)/shard_map/all_to_all | solution.py:90
  806.9 190.9 %all-reduce.11.cloned.1.call-start = ((), (), s32[]{:S(2)}) async-start(), calls=%async_computation.12 | async-start | bytes 4194304 | tf_op jit(solution)/shard_map/psum | solution.py:397
  837.4 170.0 %all-reduce.13.cloned.1.call-start = ((), (), s32[]{:S(2)}) async-start(), calls=%async_computation.14 | async-start | bytes 4194304
  837.4 12.8 %copy-start.67 = (bf16[2,576,1024]{2,1,0:T(8,128)(2,1)S(1)}, bf16[2,576,1024]{2,1,0:T(8,128)(2,1)}, u32[]{:S(2)}) copy-start(bf16[2,576,1024]{2,1,0:T(8,128)(2,1)} %copy-done.66) | copy-start | bytes 7077892
  866.6 275.3 %reduce-scatter.8.cloned.1.call-start = ((), (), s32[]{:S(2)}) async-start(), calls=%async_computation.13 | async-start | bytes 811008
  (70 other events, 322.0 us)
Sparse Core Ops, SparseCore 0:
  9.7 84.6 all-gather.3
  233.8 90.4 all-reduce.8
  390.2 52.2 all-gather.5
  462.7 51.8 reduce-scatter.5
  567.7 91.8 all-gather.7
  837.5 59.0 all-reduce.10
  899.9 107.4 all-reduce.12
  1009.7 132.1 reduce-scatter.7
where the time goes:
time: 1160 us; the launch traced here: 1150 us
  waiting for transfers between devices  409 us (35%)
  blocking collectives  337 us (29%)
  matrix products  149 us (13%)
  local copies, waits for them, and re-layouts  136 us (12%)
  other arithmetic  92.6 us (8%)
  between operations  17.1 us (1%)
  starting transfers between devices  12.2 us (1%)
    all_gather x2, waiting for transfers between devices, in_one_piece(): lax.all_gather(both, axis, axis=dim, tiled=True)  144 us
    unnamed x10, waiting for transfers between devices  130 us
    unnamed x1, blocking collectives  126 us
    all_to_all x2, blocking collectives, in_one_piece_2(): lax.all_to_all(both, axis, split_axis=split_dim, concat_axis=concat_dim,...  78.2 us
    all_gather x1, blocking collectives, on_device(): lax.all_gather(qv_bias, ('fsdp', 'ctx'), axis=2, tiled=True)  67.1 us
    all_gather x1, blocking collectives, in_one_piece(): lax.all_gather(both, axis, axis=dim, tiled=True)  65.3 us
    reduce_scatter x1, waiting for transfers between devices, in_one_piece_3(): whole = lax.psum_scatter(both, axis, scatter_dimension=dim, tiled=True)  51.3 us
    psum x1, waiting for transfers between devices, on_device(): branch = lax.psum(branch_part, 'tp') + shift_rows[2]  43.3 us
  transfers between devices with their start and end apart: 11, of which 8 were waited for; matrix products, arithmetic and copies ran while one was open for 9% of the time, Pallas kernels for 0%

commit v1 on v0

v1 whole, which is shorter than its diff:
```python
import jax
import jax.numpy as jnp
from jax import lax
from jax.experimental import pallas as pl
from jax.experimental.pallas import tpu as pltpu
from jax.sharding import PartitionSpec as P

HD = 64
EPSILON = 1e-05
NEGATIVE = -1e30
REACH = 800
SIDE = 256
FC = ("fsdp", "ctx")
BF = jnp.bfloat16
F32 = jnp.float32


def dot(a, b, ca, cb):
    return lax.dot_general(a, b, (((ca,), (cb,)), ((), ())), preferred_element_type=F32)


def by_head(cols, heads):
    row = lax.broadcasted_iota(jnp.int32, cols.shape, 0) // HD
    zero = jnp.zeros_like(cols)
    return jnp.concatenate([jnp.where(row == h, cols, zero) for h in range(heads)], axis=1)


def pair_mask(start_row, q_first, k_first):
    k_pos = lax.broadcasted_iota(jnp.int32, (SIDE, SIDE), 0) + k_first
    q_pos = lax.broadcasted_iota(jnp.int32, (SIDE, SIDE), 1) + q_first
    return (k_pos >= start_row) & (k_pos <= q_pos)


def forward_kernel(first_ref, q_ref, start_ref, k_ref, v_ref, o_ref, exact_ref, lse_ref, q_heads, acc):
    heads = q_ref.shape[0] // HD
    halo = (k_ref.shape[0] - SIDE * pl.num_programs(0)) // SIDE
    i = pl.program_id(0)
    own = halo + i
    q_heads[...] = by_head(q_ref[...] * jnp.asarray(HD**-0.5, BF), heads)
    acc[...] = jnp.zeros_like(acc)
    start_row = start_ref[...]

    def step(n, carry):
        peak, total = carry
        j = own - n
        rows = pl.ds(pl.multiple_of(j * SIDE, SIDE), SIDE)
        scores = dot(k_ref[rows, :], q_heads[...], 1, 0)
        allowed = pair_mask(start_row, own * SIDE, j * SIDE)
        scores = jnp.where(jnp.concatenate([allowed] * heads, axis=1), scores, NEGATIVE)
        new_peak = jnp.maximum(peak, jnp.max(scores, axis=0, keepdims=True))
        fade = jnp.exp(peak - new_peak)
        weights = jnp.exp(scores - new_peak)
        total = total * fade + jnp.sum(weights, axis=0, keepdims=True)
        low = weights.astype(BF)
        v_t = v_ref[rows, :].T
        for h in range(heads):
            at, cols = slice(h * HD, (h + 1) * HD), slice(h * SIDE, (h + 1) * SIDE)
            acc[at, :] = acc[at, :] * fade[:, cols] + dot(v_t[at, :], low[:, cols], 1, 0)
        return new_peak, total

    width = heads * SIDE
    peak, total = lax.fori_loop(
        0, own - first_ref[i] + 1, step, (jnp.full((1, width), NEGATIVE, F32), jnp.zeros((1, width), F32))
    )
    scale = 1.0 / total
    for h in range(heads):
        at, cols = slice(h * HD, (h + 1) * HD), slice(h * SIDE, (h + 1) * SIDE)
        exact = acc[at, :] * scale[:, cols]
        exact_ref[at, :] = exact
        o_ref[at, :] = exact.astype(BF)
    lse_ref[0] = peak + jnp.log(total)


def attend_forward(first, q_t, start, k_ext, v_ext):
    channels, rows = q_t.shape
    blocks = rows // SIDE
    width = channels // HD * SIDE
    whole = pl.BlockSpec(k_ext.shape, lambda i, f: (0, 0))
    column = pl.BlockSpec((channels, SIDE), lambda i, f: (0, i))
    return pl.pallas_call(
        forward_kernel,
        out_shape=(
            jax.ShapeDtypeStruct((channels, rows), BF),
            jax.ShapeDtypeStruct((channels, rows), F32),
            jax.ShapeDtypeStruct((blocks, 1, width), F32),
        ),
        grid_spec=pltpu.PrefetchScalarGridSpec(
            num_scalar_prefetch=1,
            grid=(blocks,),
            in_specs=[column, pl.BlockSpec((1, SIDE), lambda i, f: (0, i)), whole, whole],
            out_specs=(column, column, pl.BlockSpec((1, 1, width), lambda i, f: (i, 0, 0))),
            scratch_shapes=[pltpu.VMEM((channels, width), BF), pltpu.VMEM((channels, SIDE), F32)],
        ),
        compiler_params=pltpu.CompilerParams(vmem_limit_bytes=32 * 2**20),
        cost_estimate=pl.CostEstimate(flops=6_000_000_000, bytes_accessed=6_000_000, transcendentals=4_000_000),
        name="attend_forward",
    )(first, q_t, start, k_ext, v_ext)


def backward_kernel(low_block, first_ref, q_ref, g_ref, exact_ref, lse_ref, start_ref, k_ref, v_ref, add_ref,
                    dq_ref, dk_ref, dv_ref, q_heads, g_heads, dq_acc, dk_acc, dv_acc):
    heads = q_ref.shape[0] // HD
    i = pl.program_id(0)
    blocks = pl.num_programs(0)
    halo = 4
    own = halo + i
    q_heads[...] = by_head(q_ref[...] * jnp.asarray(HD**-0.5, BF), heads)
    grad = g_ref[...]
    g_heads[...] = by_head(grad, heads)
    product = grad.astype(F32) * exact_ref[...]
    delta = jnp.concatenate(
        [jnp.sum(product[h * HD : (h + 1) * HD, :], axis=0, keepdims=True) for h in range(heads)], axis=1
    )
    dq_acc[...] = jnp.zeros_like(dq_acc)

    @pl.when(i == 0)
    def _():
        dk_acc[...] = jnp.zeros_like(dk_acc)
        dv_acc[...] = jnp.zeros_like(dv_acc)

    start_row = start_ref[...]
    lse = lse_ref[0]
    near = low_block != 0

    def step(j, carry):
        rows = pl.ds(pl.multiple_of((j - low_block) * SIDE, SIDE), SIDE)
        k_block = k_ref[rows, :]
        scores = dot(k_block, q_heads[...], 1, 0)
        allowed = pair_mask(start_row, own * SIDE, j * SIDE)
        scores = jnp.where(jnp.concatenate([allowed] * heads, axis=1), scores, NEGATIVE)
        weights = jnp.exp(scores - lse)
        grad_weights = dot(v_ref[rows, :], g_heads[...], 1, 0)
        grad_scores = (weights * (grad_weights - delta)).astype(BF)
        dv_acc[rows, :] += dot(weights.astype(BF), g_heads[...], 1, 1)
        dk_acc[rows, :] += dot(grad_scores, q_heads[...], 1, 1)
        k_t = k_block.T
        for h in range(heads):
            at, cols = slice(h * HD, (h + 1) * HD), slice(h * SIDE, (h + 1) * SIDE)
            dq_acc[at, :] += dot(k_t[at, :], grad_scores[:, cols], 1, 0)
        return carry

    first = first_ref[i]
    if near:
        lax.fori_loop(jnp.maximum(first, low_block), own + 1, step, 0)
        dq_ref[...] = (dq_acc[...] * HD**-0.5 + add_ref[...]).T.astype(BF)
    else:
        lax.fori_loop(first, halo, step, 0)
        dq_ref[...] = dq_acc[...] * HD**-0.5

    @pl.when(i == blocks - 1)
    def _():
        dk_ref[...] = dk_acc[...].astype(BF)
        dv_ref[...] = dv_acc[...].astype(BF)


def far_kernel(first_ref, q_ref, g_ref, exact_ref, lse_ref, start_ref, k_ref, v_ref,
               dq_ref, dk_ref, dv_ref, q_heads, g_heads, dq_acc, dk_acc, dv_acc):
    backward_kernel(0, first_ref, q_ref, g_ref, exact_ref, lse_ref, start_ref, k_ref, v_ref, None,
                    dq_ref, dk_ref, dv_ref, q_heads, g_heads, dq_acc, dk_acc, dv_acc)


def near_kernel(*refs):
    backward_kernel(4, *refs)


def attend_backward(near, first, q_t, g_t, exact_t, lse, start, k_part, v_part, add=None):
    channels, rows = q_t.shape
    blocks = rows // SIDE
    width = channels // HD * SIDE
    whole = pl.BlockSpec(k_part.shape, lambda i, f: (0, 0))
    column = pl.BlockSpec((channels, SIDE), lambda i, f: (0, i))
    in_specs = [
        column, column, column,
        pl.BlockSpec((1, 1, width), lambda i, f: (i, 0, 0)),
        pl.BlockSpec((1, SIDE), lambda i, f: (0, i)),
        whole, whole,
    ]
    args = [first, q_t, g_t, exact_t, lse, start, k_part, v_part]
    if near:
        in_specs.append(column)
        args.append(add)
        dq_shape = jax.ShapeDtypeStruct((rows, channels), BF)
        dq_spec = pl.BlockSpec((SIDE, channels), lambda i, f: (i, 0))
    else:
        dq_shape = jax.ShapeDtypeStruct((channels, rows), F32)
        dq_spec = column
    return pl.pallas_call(
        near_kernel if near else far_kernel,
        out_shape=(dq_shape, jax.ShapeDtypeStruct(k_part.shape, BF), jax.ShapeDtypeStruct(k_part.shape, BF)),
        grid_spec=pltpu.PrefetchScalarGridSpec(
            num_scalar_prefetch=1,
            grid=(blocks,),
            in_specs=in_specs,
            out_specs=(dq_spec, whole, whole),
            scratch_shapes=[
                pltpu.VMEM((channels, width), BF),
                pltpu.VMEM((channels, width), BF),
                pltpu.VMEM((channels, SIDE), F32),
                pltpu.VMEM(k_part.shape, F32),
                pltpu.VMEM(k_part.shape, F32),
            ],
        ),
        compiler_params=pltpu.CompilerParams(vmem_limit_bytes=32 * 2**20),
        cost_estimate=pl.CostEstimate(flops=9_000_000_000, bytes_accessed=6_000_000, transcendentals=4_000_000),
        name="attend_near" if near else "attend_far",
    )(*args)


def normalized(values):
    centre = values - jnp.mean(values, axis=-1, keepdims=True)
    variance = jnp.mean(centre * centre, axis=-1, keepdims=True)
    inverse = lax.rsqrt(variance + EPSILON)
    return centre * inverse, inverse


def norm_backward(grad_out, normed, inverse, gain_row):
    scaled = grad_out * gain_row
    inner = jnp.mean(scaled, axis=-1, keepdims=True)
    along = jnp.mean(scaled * normed, axis=-1, keepdims=True)
    return inverse * (scaled - inner - normed * along)


def gather_rows(shard, axis, peers):
    return lax.all_to_all(jnp.broadcast_to(shard[None], (peers, *shard.shape)), axis, 0, 0, tiled=True)


def summed_on_arrival(whole, axis, peers):
    tiles = whole.reshape(peers, -1, whole.shape[-1])
    return lax.all_to_all(tiles, axis, 0, 0, tiled=True).astype(F32).sum(axis=0)


def on_device(tokens, cotangent, expert_ids, segment_ids, priority, w_qkv, w_out, norm_gains, norm_shifts,
              qv_bias, w_up, up_bias, w_down, down_bias):
    rows, model = tokens.shape
    channels = w_qkv.shape[2]
    heads = channels // HD
    seq_len = segment_ids.shape[0]
    f_count, c_count, t_count = (lax.axis_size(a) for a in ("fsdp", "ctx", "tp"))
    groups = f_count * c_count
    ctx_at, tp_at = lax.axis_index("ctx"), lax.axis_index("tp")
    held = w_up.shape[0]
    experts = held * groups
    capacity = (9 * seq_len + 8 * experts - 1) // (8 * experts)
    slots = experts * capacity
    shard = model // groups
    part = rows // t_count
    width = model // t_count
    forth = [(0, 1)]
    back = [(1, 0)]

    bias_column = jnp.pad(qv_bias.reshape(-1), (0, shard - qv_bias.size))[None]
    small = jnp.concatenate([norm_gains, norm_shifts, bias_column], axis=0).T
    small = jnp.pad(small, ((0, 0), (0, 128 - small.shape[1])))
    pack = jnp.concatenate([jnp.moveaxis(w_qkv, 0, 1).reshape(shard, 3 * channels), small], axis=1)
    earlier_ids = lax.ppermute(expert_ids + 1, "ctx", forth)[:, 0]
    packed = gather_rows(pack, FC, groups).reshape(model, -1)
    out_t = gather_rows(w_out.T, FC, groups).reshape(model, channels)
    qkv_full = packed[:, : 3 * channels]
    small = packed[:, 3 * channels : 3 * channels + 6].astype(F32)
    gain_rows = small[:, 0:2].T
    shift_rows = small[:, 2:5].T
    bias_rows = (
        small[:, 5].reshape(groups, shard)[:, : qv_bias.size].reshape(groups, 2, heads, -1)
        .transpose(1, 2, 0, 3).reshape(2, channels)
    )
    out_full = lax.all_gather(out_t.T, "tp", axis=0, tiled=True)

    owner = expert_ids[:, 0]
    rank = priority[0]
    before = (owner[None, :] == owner[:, None]) & (rank[None, :] < rank[:, None])
    carried = earlier_ids[None, :] == owner[:, None] + 1
    slot = jnp.sum(before.astype(jnp.int32), axis=1) + jnp.sum(carried.astype(jnp.int32), axis=1)
    target = jnp.where(slot < capacity, owner * capacity + slot, slots)
    place = (lax.broadcasted_iota(jnp.int32, (slots, rows), 0) == target[None, :]).astype(BF)

    def to_experts(columns):
        sent = dot(place, columns, 1, 0).astype(BF).reshape(groups, held * capacity, width)
        got = lax.all_to_all(sent, FC, 0, 0, tiled=True).reshape(f_count, c_count, held, capacity, width)
        mine = (got[:, 0] + got[:, 1]).transpose(1, 0, 2, 3).reshape(held, f_count * capacity, width)
        return lax.all_gather(mine, "tp", axis=2, tiled=True)

    def from_experts(mine):
        spread = mine.reshape(held, f_count, 1, capacity, width).transpose(1, 2, 0, 3, 4)
        spread = jnp.broadcast_to(spread, (f_count, c_count, held, capacity, width))
        got = lax.all_to_all(spread.reshape(groups, held * capacity, width), FC, 0, 0, tiled=True)
        return dot(place, got.reshape(slots, width), 0, 0).astype(BF)

    cot_columns = lax.dynamic_slice_in_dim(cotangent, tp_at * width, width, 1)
    expert_grads = to_experts(cot_columns)
    active_grad = jnp.einsum("emd,efd->emf", expert_grads, w_down, preferred_element_type=F32)

    inputs = tokens.astype(F32)
    normed_all, _ = normalized(inputs)
    first_low = (normed_all * gain_rows[0] + shift_rows[0]).astype(BF)
    k_low = dot(first_low, qkv_full[:, channels : 2 * channels], 1, 0).astype(BF)
    v_low = (dot(first_low, qkv_full[:, 2 * channels :], 1, 0) + bias_rows[1]).astype(BF)
    kv_far = lax.ppermute(jnp.concatenate([k_low[rows - REACH :], v_low[rows - REACH :]], axis=1), "ctx", forth)
    kv_far = jnp.pad(kv_far, ((rows - REACH, 0), (0, 0)))
    k_far, v_far = kv_far[:, :channels], kv_far[:, channels:]
    q_t = (dot(qkv_full[:, :channels], first_low, 0, 1) + bias_rows[0][:, None]).astype(BF)
    seg_own = lax.dynamic_slice_in_dim(segment_ids, ctx_at * rows, rows)
    start = jnp.sum((segment_ids[None, :] < seg_own[:, None]).astype(jnp.int32), axis=1)
    start = start + jnp.where(ctx_at == 0, rows, 0)
    first = start[::SIDE] // SIDE
    start = start[None, :]
    mixed_t, exact_t, lse = attend_forward(
        first, q_t, start, jnp.concatenate([k_far, k_low]), jnp.concatenate([v_far, v_low])
    )
    mixed_rows_t = lax.all_to_all(mixed_t, "tp", 1, 0, tiled=True)

    inputs_part = lax.dynamic_slice_in_dim(tokens, tp_at * part, part).astype(F32)
    cot_part = lax.dynamic_slice_in_dim(cotangent, tp_at * part, part).astype(F32)
    middle = inputs_part + (dot(mixed_rows_t, out_full, 0, 0) + shift_rows[2])
    normed_two, inverse_two = normalized(middle)
    second_low = (normed_two * gain_rows[1] + shift_rows[1]).astype(BF)
    second_columns = lax.all_to_all(second_low, "tp", 1, 0, tiled=True)

    expert_rows = to_experts(second_columns)
    hidden = (
        jnp.einsum("emd,edf->emf", expert_rows, w_up, preferred_element_type=F32)
        + up_bias.astype(F32)[:, None, :]
    )
    sigmoid_hidden = jax.nn.sigmoid(hidden)
    active_low = (hidden * sigmoid_hidden).astype(BF)
    slope = sigmoid_hidden * (1.0 + hidden * (1.0 - sigmoid_hidden))
    hidden_grad = (active_grad * slope).astype(BF)
    input_part = jnp.einsum("emf,edf->emd", hidden_grad, w_up, preferred_element_type=F32).astype(BF)
    input_low = lax.psum_scatter(input_part, "tp", scatter_dimension=2, tiled=True)
    grad_columns = from_experts(input_low)
    second_grad = lax.all_to_all(grad_columns, "tp", 0, 1, tiled=True).astype(F32)

    result_part = jnp.einsum("emf,efd->emd", active_low, w_down, preferred_element_type=F32).astype(BF)
    bias_columns = lax.dynamic_slice_in_dim(down_bias, tp_at * width, width, 1)
    result_sum = lax.psum_scatter(result_part, "tp", scatter_dimension=2, tiled=True)
    result_low = (result_sum.astype(F32) + bias_columns.astype(F32)[:, None, :]).astype(BF)
    expert_out = lax.all_to_all(from_experts(result_low), "tp", 0, 1, tiled=True)
    block_part = (middle + expert_out.astype(F32)).astype(BF)
    block_out = lax.all_gather(block_part, "tp", axis=0, tiled=True)

    w_up_grad = jnp.einsum("emd,emf->edf", expert_rows, hidden_grad, preferred_element_type=F32)
    w_down_grad = jnp.einsum("emf,emd->efd", active_low, expert_grads, preferred_element_type=F32)
    up_bias_grad = jnp.sum(hidden_grad.astype(F32), axis=1)
    down_bias_grad = jnp.sum(expert_grads.astype(F32), axis=1)

    middle_grad = cot_part + norm_backward(second_grad, normed_two, inverse_two, gain_rows[1])
    branch_low = middle_grad.astype(BF)
    grad_rows_t = dot(out_full, branch_low, 1, 1).astype(BF)
    grad_t = lax.all_to_all(grad_rows_t, "tp", 0, 1, tiled=True)
    branch_all = lax.all_gather(branch_low, "tp", axis=0, tiled=True)
    out_grad_t = dot(branch_all, mixed_t, 0, 1).astype(BF)
    out_shard = summed_on_arrival(out_grad_t, FC, groups).T

    dq_far, dk_far, dv_far = attend_backward(False, first, q_t, grad_t, exact_t, lse, start, k_far, v_far)
    kv_back = lax.ppermute(
        jnp.concatenate([dk_far[rows - REACH :], dv_far[rows - REACH :]], axis=1), "ctx", back
    )
    dq, dk, dv = attend_backward(True, first, q_t, grad_t, exact_t, lse, start, k_low, v_low, dq_far)
    kv_grad = jnp.concatenate([dk, dv], axis=1).astype(F32) + jnp.pad(kv_back, ((rows - REACH, 0), (0, 0))).astype(F32)
    stacked = jnp.concatenate([dq, kv_grad.astype(BF)], axis=1)
    first_part = dot(stacked, qkv_full, 1, 1).astype(BF)
    first_grad = lax.psum_scatter(first_part, "tp", scatter_dimension=0, tiled=True).astype(F32)
    qkv_grad = dot(first_low, stacked, 0, 0).astype(BF)
    qkv_shard = jnp.moveaxis(summed_on_arrival(qkv_grad, FC, groups).reshape(shard, 3, channels), 1, 0)

    normed_one, inverse_one = normalized(inputs_part)
    tokens_part = (middle_grad + norm_backward(first_grad, normed_one, inverse_one, gain_rows[0])).astype(BF)
    tokens_grad = lax.all_gather(tokens_part, "tp", axis=0, tiled=True)

    sums = jnp.stack([
        jnp.sum(first_grad * normed_one, axis=0),
        jnp.sum(second_grad * normed_two, axis=0),
        jnp.sum(first_grad, axis=0),
        jnp.sum(second_grad, axis=0),
        jnp.sum(branch_low.astype(F32), axis=0),
    ])
    stacked_sum = jnp.sum(stacked.astype(F32), axis=0)
    bias_sum = jnp.stack([stacked_sum[:channels], stacked_sum[2 * channels :]])
    sums = jnp.sum(lax.all_gather(sums, "tp", axis=0), axis=0)
    bias_tiles = bias_sum.reshape(2, heads, groups, -1).transpose(2, 0, 1, 3).reshape(groups, -1)
    sum_tiles = sums.reshape(-1, groups, shard).transpose(1, 0, 2).reshape(groups, -1)
    tail = jnp.concatenate([sum_tiles, bias_tiles], axis=1)
    tail = jnp.pad(tail, ((0, 0), (0, 256 - tail.shape[1]))).reshape(groups, 1, 256)
    tail = jnp.sum(lax.all_to_all(tail, FC, 0, 0, tiled=True), axis=0)[0]
    norm_shard = tail[: 5 * shard].reshape(5, shard)
    bias_shard = tail[5 * shard : 5 * shard + qv_bias.size].reshape(qv_bias.shape)
    return (block_out, tokens_grad, qkv_shard, out_shard, norm_shard[:2], norm_shard[2:], bias_shard,
            w_up_grad, up_bias_grad, w_down_grad, down_bias_grad)


def solution(mesh):
    token, weight = P(FC, None), P(None, FC)
    experts = P(FC, None, "tp"), P(FC, "tp"), P(FC, "tp", None), P(FC, None)
    shared = P(None, FC, "tp"), P("tp", FC), weight, weight, P(None, "tp", FC)
    return jax.shard_map(
        on_device,
        mesh=mesh,
        in_specs=(token, token, token, P("fsdp"), token, *shared, *experts),
        out_specs=(token, token, *shared, *experts),
        check_vma=False,
    )
```

time: 1160 us -> 586 us (0.51)
  blocking collectives: 337 us -> 74.8 us
  waiting for transfers between devices: 409 us -> 208 us
  local copies, waits for them, and re-layouts: 136 us -> 61.3 us
  starting transfers between devices: 12.2 us -> 82.8 us
  matrix products: 149 us -> 84.6 us
  other arithmetic: 92.6 us -> 31.8 us
  Pallas kernels: 0 us -> 16.9 us
    unnamed x10 -> x9, waiting for transfers between devices: 130 us -> 1.51 us
    unnamed x1 -> x0, blocking collectives: 126 us -> none
    all_gather x2 -> x1, blocking collectives: 132 us -> 12 us  [on_device(): sums = jnp.sum(lax.all_gather(sums, 'tp', axis=0), axis=0)]
    all_gather x3 -> x6, waiting for transfers between devices: 144 us -> 62.3 us  [the longest x2 30.2 us: to_experts(): return lax.all_gather(mine, 'tp', axis=2, tiled=True)]
    dot_general x26 -> x16, matrix products: 130 us -> 66.6 us  [the longest x12 38.8 us: dot(): lax.dot_general(a, b, (((ca,), (cb,)), ((), ())), preferred_element_type=...]
    all_to_all x3 -> x11, starting transfers between devices: 11.9 us -> 69.4 us  [the longest x2 17.4 us: summed_on_arrival(): return lax.all_to_all(tiles, axis, 0, 0, tiled=True).astype(F32).sum(axis=0)]
    psum x2 -> x0, waiting for transfers between devices: 43.3 us -> none  [the longest x1 43.3 us: on_device(): branch = lax.psum(branch_part, 'tp') + shift_rows[2]]
    gather x5 -> x0, local copies, waits for them, and re-layouts: 37.6 us -> none  [the longest x1 8.97 us: on_device(): expert_out = jnp.concatenate([back_rows, zero_row], axis=0)[target]]
  transfers between devices with their start and end apart: 11 -> 23, of which waited for: 8 -> 17; matrix products, arithmetic and copies ran while one was open for 9% -> 22% of each run, Pallas kernels for 0% -> 3%
where the time goes in v1:
time: 586 us; the launch traced here: 575 us
  waiting for transfers between devices  208 us (35%)
  matrix products  84.6 us (14%)
  starting transfers between devices  82.8 us (14%)
  blocking collectives  74.8 us (13%)
  local copies, waits for them, and re-layouts  61.3 us (10%)
  other arithmetic  31.8 us (5%)
  Pallas kernels  16.9 us (3%)
  between operations  15.1 us (3%)
    all_to_all x2, blocking collectives, to_experts(): lax.all_to_all(sent, FC, 0, 0, tiled=True)  51.3 us
    dot_general x12, matrix products, dot(): lax.dot_general(a, b, (((ca,), (cb,)), ((), ())), preferred_element_type=...  38.8 us
    all_to_all x2, waiting for transfers between devices, gather_rows(): lax.all_to_all(jnp.broadcast_to(shard[None], (peers, *shard.shape)), axis...  33.6 us
    all_gather x2, waiting for transfers between devices, to_experts(): return lax.all_gather(mine, 'tp', axis=2, tiled=True)  30.2 us
    reduce_scatter x1, waiting for transfers between devices, on_device(): lax.psum_scatter(input_part, 'tp', scatter_dimension=2, tiled=True)  25 us
    all_gather x1, waiting for transfers between devices, on_device(): block_out = lax.all_gather(block_part, 'tp', axis=0, tiled=True)  19.2 us
    all_to_all x2, starting transfers between devices, summed_on_arrival(): return lax.all_to_all(tiles, axis, 0, 0, tiled=True).astype(F32).sum(axis=0)  17.4 us
    reduce_scatter x1, waiting for transfers between devices, on_device(): lax.psum_scatter(result_part, 'tp', scatter_dimension=2, tiled=True)  15.6 us
  transfers between devices with their start and end apart: 23, of which 17 were waited for; matrix products, arithmetic and copies ran while one was open for 22% of the time, Pallas kernels for 3%

profile of v1, /device:TPU:0, one launch (start us, length us, event | category | flops | bytes accessed | tf_op | source)
XLA Modules:
  0.0 575.2 jit_solution(10121069935596857287)
XLA Ops:
  8.7 8.4 %all-to-all-start.2 = ((bf16[32,32,256]{2,1,0:T(8,128)(2,1)}), bf16[32,32,256]{2,1,0:T(8,128)(2,1)S(1)}, u32[]{:S(2)}, u32[]{:S(2)}) async-start(bf16[32,32,256]{2,1,0:T(8,128)(2,1)} %broadcast_in_dim.20), calls=%async_computation.2 | async-start | bytes 1048576 | tf_op jit(solution)/shard_map/all_to_all | solution.py:224
  19.7 9.6 %all-to-all-done.2 = bf16[32,32,256]{2,1,0:T(8,128)(2,1)S(1)} async-done(((bf16[32,32,256]{2,1,0:T(8,128)(2,1)}), bf16[32,32,256]{2,1,0:T(8,128)(2,1)S(1)}, u32[]{:S(2)}, u32[]{:S(2)}) %all-to-all-start.2) | async-done | bytes 524320 | tf_op jit(solution)/shard_map/all_to_all | solution.py:224
  36.6 24.0 %all-to-all-done = bf16[32,32,896]{2,1,0:T(8,128)(2,1)} async-done(((bf16[32,32,896]{2,1,0:T(8,128)(2,1)}), bf16[32,32,896]{2,1,0:T(8,128)(2,1)}, u32[]{:S(2)}, u32[]{:S(2)}) %all-to-all-start) | async-done | bytes 1835040 | tf_op jit(solution)/shard_map/all_to_all | solution.py:224
  78.5 12.7 %collective-permute-done = bf16[800,512]{1,0:T(8,128)(2,1)} collective-permute-done((bf16[800,512]{1,0:T(8,128)(2,1)S(1)}, bf16[800,512]{1,0:T(8,128)(2,1)}, u32[]{:S(2)}, u32[]{:S(2)}) %collective-permute-start) | collective-permute-done | bytes 819232 | tf_op jit(solution)/shard_map/ppermute | solution.py:297
  133.9 28.3 %all_to_all.128 = bf16[32,72,256]{2,1,0:T(8,128)(2,1)} all-to-all(bf16[32,72,256]{2,1,0:T(8,128)(2,1)S(1)} %bitcast.158), channel_id=1, replica_groups=mesh['fsdp'=16,'ctx'=2,'tp'=4] {'fsdp','ctx'}, dimensions={0} | all-to-all | bytes 2359296 | tf_op jit(solution)/shard_map/all_to_all | solution.py:278
  172.8 23.1 %all_to_all.129 = bf16[32,72,256]{2,1,0:T(8,128)(2,1)} all-to-all(bf16[32,72,256]{2,1,0:T(8,128)(2,1)S(1)} %bitcast.159), channel_id=1, replica_groups=mesh['fsdp'=16,'ctx'=2,'tp'=4] {'fsdp','ctx'}, dimensions={0} | all-to-all | bytes 2359296 | tf_op jit(solution)/shard_map/all_to_all | solution.py:278
  204.1 7.6 %fusion.53 = f32[2,576,1024]{2,1,0:T(8,128)} fusion(bf16[2,576,1024]{2,1,0:T(8,128)(2,1)} %all-gather.11.cloned.1.call-done, bf16[2,1024,1024]{2,1,0:T(8,128)(2,1)} %param.24), kind=kOutput, calls=%fused_computation.145 | convolution fusion | flops 2415919104 | bytes 11272192 | tf_op jit(solution)/shard_map/emd,edf->emf/dot_general | solution.py:320
  211.7 30.2 %all-gather.15.cloned.1.call-done = bf16[2,576,1024]{2,1,0:T(8,128)(2,1)} async-done(((bf16[2,576,256]{2,1,0:T(8,128)(2,1)}), bf16[2,576,1024]{2,1,0:T(8,128)(2,1)}) %all-gather.15.cloned.1.call-update) | async-done | bytes 2359312 | tf_op jit(solution)/shard_map/all_gather | solution.py:280
  241.9 8.6 %convert_reduce_fusion.3 = (f32[2,1024]{1,0:T(2,128)}, bf16[2,576,1024]{2,1,0:T(8,128)(2,1)S(1)}) fusion(f32[2,576,1024]{2,1,0:T(8,128)} %fusion.53, f32[2,1024]{1,0:T(2,128)S(1)} %convert_element_type.171, bf16[2,576,1024]{2,1,0:T(8,128)(2,1)} %all-gather.15.cloned.1.call-done, bf16[2,1024,1024]{2,1,0:T(8,128)(2,1)} %param.26), kind=kOutput, calls=%fused_computation.11 | convolution fusion | flops 2430072832 | bytes 13647872 | tf_op jit(solution)/shard_map/emd,efd->emf/dot_general | solution.py:290
  256.1 7.7 %convolution_convert_fusion.1 = bf16[2,576,1024]{2,1,0:T(8,128)(2,1)} fusion(bf16[2,1024,1024]{2,1,0:T(8,128)(2,1)} %param.26, f32[2,576,1024]{2,1,0:T(8,128)} %fusion.53, f32[2,1024]{1,0:T(2,128)S(1)} %convert_element_type.171), kind=kOutput, calls=%fused_computation.31 | convolution fusion | flops 2424176640 | bytes 11280384 | tf_op jit(solution)/shard_map/emf,efd->emd/dot_general | solution.py:332
  263.8 25.0 %reduce-scatter.6.cloned.1.call-done = bf16[2,576,256]{2,1,0:T(8,128)(2,1)} async-done(((bf16[2,576,1024]{2,1,0:T(8,128)(2,1)}), bf16[2,576,256]{2,1,0:T(8,128)(2,1)}) %reduce-scatter.6.cloned.1.call-update) | async-done | bytes 589840 | tf_op jit(solution)/shard_map/reduce_scatter | solution.py:328
  307.7 15.6 %reduce-scatter.4.cloned.1.call-done = bf16[2,576,256]{2,1,0:T(8,128)(2,1)} async-done(((bf16[2,576,1024]{2,1,0:T(8,128)(2,1)}), bf16[2,576,256]{2,1,0:T(8,128)(2,1)}) %reduce-scatter.4.cloned.1.call-update) | async-done | bytes 589840 | tf_op jit(solution)/shard_map/reduce_scatter | solution.py:334
  334.1 7.6 %all-to-all-start.5 = ((bf16[32,72,256]{2,1,0:T(8,128)(2,1)}), bf16[32,72,256]{2,1,0:T(8,128)(2,1)}, u32[]{:S(2)}, u32[]{:S(2)}) async-start(bf16[32,72,256]{2,1,0:T(8,128)(2,1)} %copy.136), calls=%async_computation.6 | async-start | bytes 2359296 | tf_op jit(solution)/shard_map/all_to_all | solution.py:285
  346.5 13.7 %all-to-all-done.5 = bf16[32,72,256]{2,1,0:T(8,128)(2,1)} async-done(((bf16[32,72,256]{2,1,0:T(8,128)(2,1)}), bf16[32,72,256]{2,1,0:T(8,128)(2,1)}, u32[]{:S(2)}, u32[]{:S(2)}) %all-to-all-start.5) | async-done | bytes 1179680 | tf_op jit(solution)/shard_map/all_to_all | solution.py:285
  395.8 11.5 %all_to_all.130 = bf16[4,256,256]{2,1,0:T(8,128)(2,1)S(1)} all-to-all(bf16[4,256,256]{2,1,0:T(8,128)(2,1)} %bitcast.155), channel_id=1, replica_groups=mesh['fsdp'=16,'ctx'=2,'tp'=4] {'tp'}, dimensions={0} | all-to-all | bytes 1048576 | tf_op jit(solution)/shard_map/all_to_all | solution.py:348
  412.1 8.7 %attend_near.1 = (bf16[1024,256]{1,0:T(8,128)(2,1)S(1)}, bf16[1024,256]{1,0:T(8,128)(2,1)S(1)}, bf16[1024,256]{1,0:T(8,128)(2,1)S(1)}) custom-call(s32[4]{0:T(128)S(1)} %and_select_fusion.first_ref.refs_0_, bf16[256,1024]{1,0:T(8,128)(2,1)S(1)} %fusion.22.q_ref.refs_1_, bf16[256,1024]{1,0:T(8,128)(2,1)S(1)} %bitcast.138, f32[256,1024]{1,0:T(8,128)S(1)} %copy-done.2, ...), custom_call_target="tpu_custom_call" | custom-call | flops 8999999488 | bytes 6000000 | tf_op jit(solution)/shard_map/attend_near/pallas_call | solution.py:187
  420.9 7.6 %collective-permute-done.2 = bf16[800,512]{1,0:T(8,128)(2,1)S(1)} collective-permute-done((bf16[800,512]{1,0:T(8,128)(2,1)S(1)}, bf16[800,512]{1,0:T(8,128)(2,1)S(1)}, u32[]{:S(2)}, u32[]{:S(2)}) %collective-permute-start.2) | collective-permute-done | bytes 819232 | tf_op jit(solution)/shard_map/ppermute | solution.py:354
  443.5 10.1 %all-to-all-start.11 = ((bf16[32,32,768]{2,1,0:T(8,128)(2,1)}), bf16[32,32,768]{2,1,0:T(8,128)(2,1)}, u32[]{:S(2)}, u32[]{:S(2)}) async-start(bf16[32,32,768]{2,1,0:T(8,128)(2,1)} %bitcast.157), calls=%async_computation.14 | async-start | bytes 3145728 | tf_op jit(solution)/shard_map/all_to_all | solution.py:229
  454.0 11.4 %reduce-scatter.8.cloned.1.call-done = bf16[256,1024]{1,0:T(8,128)(2,1)} async-done(((bf16[1024,1024]{1,0:T(8,128)(2,1)}), bf16[256,1024]{1,0:T(8,128)(2,1)}) %reduce-scatter.8.cloned.1.call-update) | async-done | bytes 524304 | tf_op jit(solution)/shard_map/reduce_scatter | solution.py:361
  469.7 9.4 %fusion.54 = f32[2,1024,1024]{2,1,0:T(8,128)} fusion(bf16[2,576,1024]{2,1,0:T(8,128)(2,1)} %all-gather.11.cloned.1.call-done, bf16[2,576,1024]{2,1,0:T(8,128)(2,1)} %copy-done.22), kind=kOutput, calls=%fused_computation.146 | convolution fusion | flops 2415919104 | bytes 13107200 | tf_op jit(solution)/shard_map/emd,emf->edf/dot_general | solution.py:340
  479.1 8.6 %fusion.47 = f32[2,1024,1024]{2,1,0:T(8,128)} fusion(bf16[2,576,1024]{2,1,0:T(8,128)(2,1)S(1)} %copy-done.12, f32[2,576,1024]{2,1,0:T(8,128)} %fusion.53, f32[2,1024]{1,0:T(2,128)S(1)} %convert_element_type.171), kind=kOutput, calls=%fused_computation.139 | convolution fusion | flops 2422996992 | bytes 15474688 | tf_op jit(solution)/shard_map/emf,emd->efd/dot_general | solution.py:341
  487.9 9.8 %all-gather.19.cloned.1.call-done = bf16[1024,1024]{1,0:T(8,128)(2,1)} async-done(((bf16[256,1024]{1,0:T(8,128)(2,1)}), bf16[1024,1024]{1,0:T(8,128)(2,1)}) %all-gather.19.cloned.1.call-update) | async-done | bytes 2097168 | tf_op jit(solution)/shard_map/all_gather | solution.py:349
  511.3 19.2 %all-gather.13.cloned.1.call-done = bf16[1024,1024]{1,0:T(8,128)(2,1)} async-done(((bf16[256,1024]{1,0:T(8,128)(2,1)}), bf16[1024,1024]{1,0:T(8,128)(2,1)}) %all-gather.13.cloned.1.call-update) | async-done | bytes 2097168 | tf_op jit(solution)/shard_map/all_gather | solution.py:338
  530.5 12.0 %all-gather.1 = f32[4,5,1024]{2,1,0:T(8,128)S(1)} all-gather(f32[1,5,1024]{2,1,0:T(8,128)S(1)} %bitcast.166), channel_id=2, replica_groups=mesh['fsdp'=16,'ctx'=2,'tp'=4] {'tp'}, dimensions={0}, use_global_device_ids=true | all-gather | bytes 102400 | tf_op jit(solution)/shard_map/all_gather | solution.py:378
  (231 shorter events, 229.6 us)
Async XLA Ops:
  8.7 20.5 %all-to-all-start.2 = ((bf16[32,32,256]{2,1,0:T(8,128)(2,1)}), bf16[32,32,256]{2,1,0:T(8,128)(2,1)S(1)}, u32[]{:S(2)}, u32[]{:S(2)}) async-start(bf16[32,32,256]{2,1,0:T(8,128)(2,1)} %broadcast_in_dim.20), calls=%async_computation.2 | async-start | bytes 1048576 | tf_op jit(solution)/shard_map/all_to_all | solution.py:224
  30.7 29.9 %all-to-all-start = ((bf16[32,32,896]{2,1,0:T(8,128)(2,1)}), bf16[32,32,896]{2,1,0:T(8,128)(2,1)}, u32[]{:S(2)}, u32[]{:S(2)}) async-start(bf16[32,32,896]{2,1,0:T(8,128)(2,1)} %broadcast_in_dim.19), calls=%async_computation | async-start | bytes 3670016 | tf_op jit(solution)/shard_map/all_to_all | solution.py:224
  35.4 78.6 %all-gather.9.cloned.1.call-start = ((), (), s32[]{:S(2)}) async-start(), calls=%async_computation.17 | async-start | bytes 2621440 | tf_op jit(solution)/shard_map/all_gather | solution.py:266
  70.8 20.4 %collective-permute-start = (bf16[800,512]{1,0:T(8,128)(2,1)S(1)}, bf16[800,512]{1,0:T(8,128)(2,1)}, u32[]{:S(2)}, u32[]{:S(2)}) collective-permute-start(bf16[800,512]{1,0:T(8,128)(2,1)S(1)} %pad_maximum_fusion.3), channel_id=1, source_target_pairs={{0,4},{1,5},{2,6},{3,7},{8,12},{9,13},{10,14},{11,15},{16,20},{17,... | collective-permute-start | bytes 2457608 | tf_op jit(solution)/shard_map/ppermute | solution.py:297
  100.9 13.1 %all-to-all-start.1 = ((bf16[256,4,256]{2,0,1:T(8,128)(2,1)}), bf16[256,4,256]{2,0,1:T(8,128)(2,1)}, u32[]{:S(2)}, u32[]{:S(2)}) async-start(bf16[256,4,256]{2,0,1:T(8,128)(2,1)} %bitcast.152), calls=%async_computation.1 | async-start | bytes 1048576 | tf_op jit(solution)/shard_map/all_to_all | solution.py:309
  105.2 19.0 %collective-permute-start.1 = (s32[1024,1]{0,1:T(1,128)S(1)}, s32[1024,1]{0,1:T(1,128)S(1)}, u32[]{:S(2)}, u32[]{:S(2)}) collective-permute-start(s32[1024,1]{0,1:T(1,128)S(1)} %broadcast_add_fusion), channel_id=1, source_target_pairs={{0,4},{1,5},{2,6},{3,7},{8,12},{9,13},{10,14},{11,15},{16,20},{17,... | collective-permute-start | bytes 12296 | tf_op jit(solution)/shard_map/ppermute | solution.py:255
  118.8 12.3 %all-to-all-start.3 = ((bf16[256,4,256]{2,0,1:T(8,128)(2,1)}), bf16[256,4,256]{2,0,1:T(8,128)(2,1)}, u32[]{:S(2)}, u32[]{:S(2)}) async-start(bf16[256,4,256]{2,0,1:T(8,128)(2,1)} %bitcast.153), calls=%async_computation.3 | async-start | bytes 1048576 | tf_op jit(solution)/shard_map/all_to_all | solution.py:316
  122.9 81.2 %all-gather.11.cloned.1.call-start = ((), (), s32[]{:S(2)}) async-start(), calls=%async_computation.18 | async-start | bytes 2949120 | tf_op jit(solution)/shard_map/all_gather | solution.py:280
  169.9 72.1 %all-gather.15.cloned.1.call-start = ((), (), s32[]{:S(2)}) async-start(), calls=%async_computation.21 | async-start | bytes 2949120 | tf_op jit(solution)/shard_map/all_gather | solution.py:280
  203.6 85.3 %reduce-scatter.6.cloned.1.call-start = ((), (), s32[]{:S(2)}) async-start(), calls=%async_computation.22 | async-start | bytes 2949120 | tf_op jit(solution)/shard_map/reduce_scatter | solution.py:328
  255.9 67.4 %reduce-scatter.4.cloned.1.call-start = ((), (), s32[]{:S(2)}) async-start(), calls=%async_computation.19 | async-start | bytes 2949120 | tf_op jit(solution)/shard_map/reduce_scatter | solution.py:334
  299.6 34.5 %all-to-all-start.8 = ((bf16[32,72,256]{2,1,0:T(8,128)(2,1)}), bf16[32,72,256]{2,1,0:T(8,128)(2,1)}, u32[]{:S(2)}, u32[]{:S(2)}) async-start(bf16[32,72,256]{2,1,0:T(8,128)(2,1)} %copy.143), calls=%async_computation.10 | async-start | bytes 2359296 | tf_op jit(solution)/shard_map/all_to_all | solution.py:285
  334.1 26.0 %all-to-all-start.5 = ((bf16[32,72,256]{2,1,0:T(8,128)(2,1)}), bf16[32,72,256]{2,1,0:T(8,128)(2,1)}, u32[]{:S(2)}, u32[]{:S(2)}) async-start(bf16[32,72,256]{2,1,0:T(8,128)(2,1)} %copy.136), calls=%async_computation.6 | async-start | bytes 2359296 | tf_op jit(solution)/shard_map/all_to_all | solution.py:285
  360.2 13.5 %all-to-all-start.9 = ((bf16[4,256,256]{2,1,0:T(8,128)(2,1)}), bf16[4,256,256]{2,1,0:T(8,128)(2,1)}, u32[]{:S(2)}, u32[]{:S(2)}) async-start(bf16[4,256,256]{2,1,0:T(8,128)(2,1)} %bitcast.162), calls=%async_computation.11 | async-start | bytes 1048576 | tf_op jit(solution)/shard_map/all_to_all | solution.py:330
  373.6 12.3 %all-to-all-start.6 = ((bf16[4,256,256]{2,1,0:T(8,128)(2,1)}), bf16[4,256,256]{2,1,0:T(8,128)(2,1)}, u32[]{:S(2)}, u32[]{:S(2)}) async-start(bf16[4,256,256]{2,1,0:T(8,128)(2,1)} %bitcast.161), calls=%async_computation.7 | async-start | bytes 1048576 | tf_op jit(solution)/shard_map/all_to_all | solution.py:336
  377.8 87.6 %reduce-scatter.8.cloned.1.call-start = ((), (), s32[]{:S(2)}) async-start(), calls=%async_computation.23 | async-start | bytes 2621440 | tf_op jit(solution)/shard_map/reduce_scatter | solution.py:361
  410.4 18.0 %collective-permute-start.2 = (bf16[800,512]{1,0:T(8,128)(2,1)S(1)}, bf16[800,512]{1,0:T(8,128)(2,1)S(1)}, u32[]{:S(2)}, u32[]{:S(2)}) collective-permute-start(bf16[800,512]{1,0:T(8,128)(2,1)S(1)} %pad_maximum_fusion.4), channel_id=1, source_target_pairs={{4,0},{5,1},{6,2},{7,3},{12,8},{13,9},{14,10},{15,11},{20,16},{21,... | collective-permute-start | bytes 2457608 | tf_op jit(solution)/shard_map/ppermute | solution.py:354
  433.6 64.2 %all-gather.19.cloned.1.call-start = ((), (), s32[]{:S(2)}) async-start(), calls=%async_computation.25 | async-start | bytes 2621440 | tf_op jit(solution)/shard_map/all_gather | solution.py:349
  434.4 96.1 %all-gather.13.cloned.1.call-start = ((), (), s32[]{:S(2)}) async-start(), calls=%async_computation.20 | async-start | bytes 2621440 | tf_op jit(solution)/shard_map/all_gather | solution.py:338
  443.5 23.7 %copy-start.9 = (f32[256,1024]{1,0:T(8,128)S(1)}, f32[256,1024]{1,0:T(8,128)}, u32[]{:S(2)}) copy-start(f32[256,1024]{1,0:T(8,128)} %get-tuple-element.99) | copy-start | bytes 3145732
  443.5 57.5 %all-to-all-start.11 = ((bf16[32,32,768]{2,1,0:T(8,128)(2,1)}), bf16[32,32,768]{2,1,0:T(8,128)(2,1)}, u32[]{:S(2)}, u32[]{:S(2)}) async-start(bf16[32,32,768]{2,1,0:T(8,128)(2,1)} %bitcast.157), calls=%async_computation.14 | async-start | bytes 3145728 | tf_op jit(solution)/shard_map/all_to_all | solution.py:229
  453.6 110.0 %all-gather.17.cloned.1.call-start = ((), (), s32[]{:S(2)}) async-start(), calls=%async_computation.24 | async-start | bytes 2621440 | tf_op jit(solution)/shard_map/all_gather | solution.py:367
  501.0 42.5 %all-to-all-start.12 = ((bf16[32,32,256]{2,1,0:T(8,128)(2,1)}), bf16[32,32,256]{2,1,0:T(8,128)(2,1)S(1)}, u32[]{:S(2)}, u32[]{:S(2)}) async-start(bf16[32,32,256]{2,1,0:T(8,128)(2,1)} %bitcast.44), calls=%async_computation.15 | async-start | bytes 1048576 | tf_op jit(solution)/shard_map/all_to_all | solution.py:229
  543.5 14.8 %all-to-all-start.13 = ((f32[32,1,256]{2,1,0:T(1,128)}), f32[32,1,256]{2,1,0:T(1,128)S(1)}, u32[]{:S(2)}, u32[]{:S(2)}) async-start(f32[32,1,256]{2,1,0:T(1,128)} %reshape.262), calls=%async_computation.16 | async-start | bytes 65536 | tf_op jit(solution)/shard_map/all_to_all | solution.py:383
  (23 other events, 108.9 us)
Sparse Core Ops, SparseCore 0:
  38.5 35.8 all-gather.8
  170.0 32.0 all-gather.10
  204.3 37.6 all-gather.14
  256.0 32.7 reduce-scatter.5
  291.7 31.5 reduce-scatter.3
  433.7 31.6 reduce-scatter.7
  467.2 30.5 all-gather.18
  499.5 30.8 all-gather.12
  532.8 30.8 all-gather.16

commit v2 on v1

v2 whole, which is shorter than its diff:
```python
import functools

import jax
import jax.numpy as jnp
from jax import lax
from jax.experimental import pallas as pl
from jax.experimental.pallas import tpu as pltpu
from jax.sharding import Mesh, PartitionSpec as P

HD = 64
EPSILON = 1e-05
NEGATIVE = -1e30
REACH = 800
SIDE = 256
FC = ("y_hi", "z", "core", "ctx")
Y = ("y_hi", "ctx")
PARTS = 4
VMEM = 40 * 2**20
BF = jnp.bfloat16
F32 = jnp.float32


def dot(a, b, ca, cb):
    return lax.dot_general(a, b, (((ca,), (cb,)), ((), ())), preferred_element_type=F32)


def by_head(cols, heads):
    row = lax.broadcasted_iota(jnp.int32, cols.shape, 0) // HD
    zero = jnp.zeros_like(cols)
    return jnp.concatenate([jnp.where(row == h, cols, zero) for h in range(heads)], axis=1)


def pair_mask(start_row, q_first, k_first):
    k_pos = lax.broadcasted_iota(jnp.int32, (SIDE, SIDE), 0) + k_first
    q_pos = lax.broadcasted_iota(jnp.int32, (SIDE, SIDE), 1) + q_first
    return (k_pos >= start_row) & (k_pos <= q_pos)


def forward_kernel(at_ref, q_ref, start_ref, k_ref, v_ref, o_ref, exact_ref, lse_ref, q_heads, acc):
    heads = q_ref.shape[0] // HD
    i = pl.program_id(0)
    own = k_ref.shape[0] // SIDE - pl.num_programs(0) + i
    q_heads[...] = by_head(q_ref[...] * jnp.asarray(HD**-0.5, BF), heads)
    acc[...] = jnp.zeros_like(acc)
    start_row = start_ref[...]

    def step(n, carry):
        peak, total = carry
        j = own - n
        rows = pl.ds(pl.multiple_of(j * SIDE, SIDE), SIDE)
        scores = dot(k_ref[rows, :], q_heads[...], 1, 0)
        allowed = pair_mask(start_row, own * SIDE, j * SIDE)
        scores = jnp.where(jnp.concatenate([allowed] * heads, axis=1), scores, NEGATIVE)
        new_peak = jnp.maximum(peak, jnp.max(scores, axis=0, keepdims=True))
        fade = jnp.exp(peak - new_peak)
        weights = jnp.exp(scores - new_peak)
        total = total * fade + jnp.sum(weights, axis=0, keepdims=True)
        low = weights.astype(BF)
        v_t = v_ref[rows, :].T
        for h in range(heads):
            at, cols = slice(h * HD, (h + 1) * HD), slice(h * SIDE, (h + 1) * SIDE)
            acc[at, :] = acc[at, :] * fade[:, cols] + dot(v_t[at, :], low[:, cols], 1, 0)
        return new_peak, total

    width = heads * SIDE
    peak, total = lax.fori_loop(
        0, own - at_ref[i] + 1, step, (jnp.full((1, width), NEGATIVE, F32), jnp.zeros((1, width), F32))
    )
    scale = 1.0 / total
    for h in range(heads):
        at, cols = slice(h * HD, (h + 1) * HD), slice(h * SIDE, (h + 1) * SIDE)
        exact = acc[at, :] * scale[:, cols]
        exact_ref[at, :] = exact
        o_ref[at, :] = exact.astype(BF)
    lse_ref[0] = peak + jnp.log(total)


def turned(i, at):
    return lax.rem(i + PARTS - at[PARTS], PARTS)


def attend_forward(at, q_t, start, k_ext, v_ext):
    channels, rows = q_t.shape
    blocks = rows // SIDE
    width = channels // HD * SIDE
    whole = pl.BlockSpec(k_ext.shape, lambda i, f: (0, 0))
    column = pl.BlockSpec((channels, SIDE), lambda i, f: (0, i))
    return pl.pallas_call(
        forward_kernel,
        out_shape=(
            jax.ShapeDtypeStruct((channels, rows), BF),
            jax.ShapeDtypeStruct((channels, rows), F32),
            jax.ShapeDtypeStruct((blocks, 1, width), F32),
        ),
        grid_spec=pltpu.PrefetchScalarGridSpec(
            num_scalar_prefetch=1,
            grid=(blocks,),
            in_specs=[column, pl.BlockSpec((1, SIDE), lambda i, f: (0, i)), whole, whole],
            out_specs=(
                pl.BlockSpec((channels, SIDE), lambda i, f: (0, turned(i, f))),
                column,
                pl.BlockSpec((1, 1, width), lambda i, f: (i, 0, 0)),
            ),
            scratch_shapes=[pltpu.VMEM((channels, width), BF), pltpu.VMEM((channels, SIDE), F32)],
        ),
        compiler_params=pltpu.CompilerParams(vmem_limit_bytes=VMEM),
        cost_estimate=pl.CostEstimate(flops=6_000_000_000, bytes_accessed=6_000_000, transcendentals=4_000_000),
        name="attend_forward",
    )(at, q_t, start, k_ext, v_ext)


def backward_kernel(low_block, at_ref, q_ref, g_ref, exact_ref, lse_ref, start_ref, k_ref, v_ref, add_ref,
                    dq_ref, dk_ref, dv_ref, q_heads, g_heads, dq_acc, dk_acc, dv_acc):
    heads = q_ref.shape[0] // HD
    i = pl.program_id(0)
    blocks = pl.num_programs(0)
    halo = PARTS
    own = halo + i
    q_heads[...] = by_head(q_ref[...] * jnp.asarray(HD**-0.5, BF), heads)
    grad = g_ref[...]
    g_heads[...] = by_head(grad, heads)
    product = grad.astype(F32) * exact_ref[...]
    delta = jnp.concatenate(
        [jnp.sum(product[h * HD : (h + 1) * HD, :], axis=0, keepdims=True) for h in range(heads)], axis=1
    )
    dq_acc[...] = jnp.zeros_like(dq_acc)

    @pl.when(i == 0)
    def _():
        dk_acc[...] = jnp.zeros_like(dk_acc)
        dv_acc[...] = jnp.zeros_like(dv_acc)

    start_row = start_ref[...]
    lse = lse_ref[0]

    def step(j, carry):
        rows = pl.ds(pl.multiple_of((j - low_block) * SIDE, SIDE), SIDE)
        k_block = k_ref[rows, :]
        scores = dot(k_block, q_heads[...], 1, 0)
        allowed = pair_mask(start_row, own * SIDE, j * SIDE)
        scores = jnp.where(jnp.concatenate([allowed] * heads, axis=1), scores, NEGATIVE)
        weights = jnp.exp(scores - lse)
        grad_weights = dot(v_ref[rows, :], g_heads[...], 1, 0)
        grad_scores = (weights * (grad_weights - delta)).astype(BF)
        dv_acc[rows, :] += dot(weights.astype(BF), g_heads[...], 1, 1)
        dk_acc[rows, :] += dot(grad_scores, q_heads[...], 1, 1)
        k_t = k_block.T
        for h in range(heads):
            at, cols = slice(h * HD, (h + 1) * HD), slice(h * SIDE, (h + 1) * SIDE)
            dq_acc[at, :] += dot(k_t[at, :], grad_scores[:, cols], 1, 0)
        return carry

    first = at_ref[i]
    if low_block:
        lax.fori_loop(jnp.maximum(first, low_block), own + 1, step, 0)
        dq_ref[...] = (dq_acc[...] * HD**-0.5 + add_ref[...]).T.astype(BF)
    else:
        lax.fori_loop(first, halo, step, 0)
        dq_ref[...] = dq_acc[...] * HD**-0.5

    @pl.when(i == blocks - 1)
    def _():
        dk_ref[...] = dk_acc[...].astype(BF)
        dv_ref[...] = dv_acc[...].astype(BF)


def far_kernel(at_ref, q_ref, g_ref, exact_ref, lse_ref, start_ref, k_ref, v_ref, *rest):
    backward_kernel(0, at_ref, q_ref, g_ref, exact_ref, lse_ref, start_ref, k_ref, v_ref, None, *rest)


def near_kernel(*refs):
    backward_kernel(PARTS, *refs)


def attend_backward(near, at, q_t, g_t, exact_t, lse, start, k_part, v_part, add=None):
    channels, rows = q_t.shape
    blocks = rows // SIDE
    width = channels // HD * SIDE
    whole = pl.BlockSpec(k_part.shape, lambda i, f: (0, 0))
    column = pl.BlockSpec((channels, SIDE), lambda i, f: (0, i))
    in_specs = [
        column,
        pl.BlockSpec((channels, SIDE), lambda i, f: (0, turned(i, f))),
        column,
        pl.BlockSpec((1, 1, width), lambda i, f: (i, 0, 0)),
        pl.BlockSpec((1, SIDE), lambda i, f: (0, i)),
        whole, whole,
    ]
    args = [at, q_t, g_t, exact_t, lse, start, k_part, v_part]
    if near:
        in_specs.append(column)
        args.append(add)
        dq_shape = jax.ShapeDtypeStruct((rows, channels), BF)
        dq_spec = pl.BlockSpec((SIDE, channels), lambda i, f: (i, 0))
    else:
        dq_shape = jax.ShapeDtypeStruct((channels, rows), F32)
        dq_spec = column
    return pl.pallas_call(
        near_kernel if near else far_kernel,
        out_shape=(dq_shape, jax.ShapeDtypeStruct(k_part.shape, BF), jax.ShapeDtypeStruct(k_part.shape, BF)),
        grid_spec=pltpu.PrefetchScalarGridSpec(
            num_scalar_prefetch=1,
            grid=(blocks,),
            in_specs=in_specs,
            out_specs=(dq_spec, whole, whole),
            scratch_shapes=[
                pltpu.VMEM((channels, width), BF),
                pltpu.VMEM((channels, width), BF),
                pltpu.VMEM((channels, SIDE), F32),
                pltpu.VMEM(k_part.shape, F32),
                pltpu.VMEM(k_part.shape, F32),
            ],
        ),
        compiler_params=pltpu.CompilerParams(vmem_limit_bytes=VMEM),
        cost_estimate=pl.CostEstimate(flops=9_000_000_000, bytes_accessed=6_000_000, transcendentals=4_000_000),
        name="attend_near" if near else "attend_far",
    )(*args)


def slots_kernel(target_ref, x_ref, o_ref):
    place = lax.broadcasted_iota(jnp.int32, (o_ref.shape[0], x_ref.shape[0]), 0) + pl.program_id(0) * o_ref.shape[0]
    o_ref[...] = dot((place == target_ref[...]).astype(F32).astype(BF), x_ref[...], 1, 0).astype(BF)


def to_slots(target, x, slots):
    return pl.pallas_call(
        slots_kernel,
        out_shape=jax.ShapeDtypeStruct((slots, x.shape[1]), BF),
        grid=(slots // SIDE,),
        in_specs=[pl.BlockSpec((1, x.shape[0]), lambda i: (0, 0)), pl.BlockSpec(x.shape, lambda i: (0, 0))],
        out_specs=pl.BlockSpec((SIDE, x.shape[1]), lambda i: (i, 0)),
        compiler_params=pltpu.CompilerParams(vmem_limit_bytes=VMEM),
        cost_estimate=pl.CostEstimate(flops=1_200_000_000, bytes_accessed=2_000_000, transcendentals=0),
        name="to_slots",
    )(target[None, :], x)


def tokens_kernel(target_ref, x_ref, o_ref):
    place = lax.broadcasted_iota(jnp.int32, (o_ref.shape[0], x_ref.shape[0]), 1)
    o_ref[...] = dot((place == target_ref[...]).astype(F32).astype(BF), x_ref[...], 1, 0).astype(BF)


def to_tokens(target, x):
    rows = target.shape[0]
    return pl.pallas_call(
        tokens_kernel,
        out_shape=jax.ShapeDtypeStruct((rows, x.shape[1]), BF),
        grid=(rows // SIDE,),
        in_specs=[pl.BlockSpec((SIDE, 1), lambda i: (i, 0)), pl.BlockSpec(x.shape, lambda i: (0, 0))],
        out_specs=pl.BlockSpec((SIDE, x.shape[1]), lambda i: (i, 0)),
        compiler_params=pltpu.CompilerParams(vmem_limit_bytes=VMEM),
        cost_estimate=pl.CostEstimate(flops=1_200_000_000, bytes_accessed=2_000_000, transcendentals=0),
        name="to_tokens",
    )(target[:, None], x)


def join_kernel(got_ref, o_ref, held):
    capacity = got_ref.shape[1] // o_ref.shape[0]
    for f in range(got_ref.shape[0] // 2):
        both = got_ref[2 * f].astype(F32) + got_ref[2 * f + 1].astype(F32)
        for e in range(o_ref.shape[0]):
            held[e, f * capacity : (f + 1) * capacity, :] = both[e * capacity : (e + 1) * capacity, :]
    o_ref[...] = held[...].astype(BF)


def join(got, experts):
    shape = (experts, got.shape[0] // 2 * (got.shape[1] // experts), got.shape[2])
    return pl.pallas_call(
        join_kernel,
        out_shape=jax.ShapeDtypeStruct(shape, BF),
        scratch_shapes=[pltpu.VMEM(shape, F32)],
        compiler_params=pltpu.CompilerParams(vmem_limit_bytes=VMEM),
        cost_estimate=pl.CostEstimate(flops=600_000, bytes_accessed=2_000_000, transcendentals=0),
        name="join",
    )(got)


def spread_kernel(bias_ref, *refs):
    o_ref, held, piece = refs[-3:]
    experts = held.shape[0]
    capacity = o_ref.shape[1] // experts
    for e in range(experts):
        total = refs[e * PARTS][...].astype(F32)
        for s in range(1, PARTS):
            total += refs[e * PARTS + s][...].astype(F32)
        held[e] = total + bias_ref[e : e + 1, :]
    for f in range(o_ref.shape[0] // 2):
        for e in range(experts):
            piece[e * capacity : (e + 1) * capacity, :] = held[e, f * capacity : (f + 1) * capacity, :]
        low = piece[...].astype(BF)
        o_ref[2 * f] = low
        o_ref[2 * f + 1] = low


def spread(parts, bias, capacity):
    experts = len(parts)
    rows, n = parts[0][0].shape
    return pl.pallas_call(
        spread_kernel,
        out_shape=jax.ShapeDtypeStruct((rows // capacity * 2, experts * capacity, n), BF),
        scratch_shapes=[pltpu.VMEM((experts, rows, n), F32), pltpu.VMEM((experts * capacity, n), F32)],
        compiler_params=pltpu.CompilerParams(vmem_limit_bytes=VMEM),
        cost_estimate=pl.CostEstimate(flops=2_400_000, bytes_accessed=4_000_000, transcendentals=0),
        name="spread",
    )(bias, *[p for e in parts for p in e])


def expert_kernel(at_ref, r0, r1, r2, r3, w_ref, b_ref, g_ref, act_ref, hg_ref, o_ref, acc):
    rows = (r0, r1, r2, r3)
    n = r0.shape[1]
    j = pl.program_id(0)

    def weights(s):
        place = lax.rem(at_ref[PARTS] + PARTS - s, PARTS)
        return w_ref[0, pl.ds(pl.multiple_of(place * n, n), n), :]

    hidden = b_ref[0].astype(F32)
    for s in range(PARTS):
        hidden = hidden + dot(rows[s][...], weights(s), 1, 0)
    gate = jax.nn.sigmoid(hidden)
    act_ref[...] = (hidden * gate).astype(BF)
    grad = (g_ref[...] * (gate * (1.0 + hidden * (1.0 - gate)))).astype(BF)
    hg_ref[...] = grad

    for s in range(PARTS):
        here = dot(grad, weights(s), 1, 1)

        @pl.when(j == 0)
        def _():
            acc[s] = here

        @pl.when(j > 0)
        def _():
            acc[s] += here

    @pl.when(j == pl.num_programs(0) - 1)
    def _():
        o_ref[...] = acc[...].astype(BF)


def run_expert(e, at, parts, w_up, up_bias, active_grad):
    rows, n = parts[0].shape
    inner = w_up.shape[2]
    whole = pl.BlockSpec((rows, n), lambda j, f: (0, 0))
    block = pl.BlockSpec((rows, SIDE), lambda j, f: (0, j))
    return pl.pallas_call(
        expert_kernel,
        out_shape=(
            jax.ShapeDtypeStruct((rows, inner), BF),
            jax.ShapeDtypeStruct((rows, inner), BF),
            jax.ShapeDtypeStruct((PARTS, rows, n), BF),
        ),
        grid_spec=pltpu.PrefetchScalarGridSpec(
            num_scalar_prefetch=1,
            grid=(inner // SIDE,),
            in_specs=[whole] * PARTS + [
                pl.BlockSpec((1, w_up.shape[1], SIDE), lambda j, f: (e, 0, j)),
                pl.BlockSpec((1, 1, SIDE), lambda j, f: (e, 0, j)),
                block,
            ],
            out_specs=(block, block, pl.BlockSpec((PARTS, rows, n), lambda j, f: (0, 0, 0))),
            scratch_shapes=[pltpu.VMEM((PARTS, rows, n), F32)],
        ),
        compiler_params=pltpu.CompilerParams(vmem_limit_bytes=VMEM),
        cost_estimate=pl.CostEstimate(flops=2_400_000_000, bytes_accessed=8_000_000, transcendentals=600_000),
        name="expert",
    )(at, *parts, w_up, up_bias[:, None, :], active_grad)


def place_kernel(axis, step, at_ref, *refs):
    parts, o_ref, sems = refs[:-2], refs[-2], refs[-1]
    copies = []
    for s, part in enumerate(parts):
        place = lax.rem(at_ref[PARTS] + step * s + PARTS, PARTS)
        n = part.shape[axis]
        window = pl.ds(pl.multiple_of(place * n, n), n)
        target = o_ref.at[window, :] if axis == 0 else o_ref.at[:, window]
        copies.append(pltpu.make_async_copy(part, target, sems.at[s]))
    for copy in copies:
        copy.start()
    for copy in copies:
        copy.wait()


def placed(at, parts, axis, step):
    shape = list(parts[0].shape)
    shape[axis] *= PARTS
    hbm = pl.BlockSpec(memory_space=pl.ANY)
    return pl.pallas_call(
        functools.partial(place_kernel, axis, step),
        out_shape=jax.ShapeDtypeStruct(tuple(shape), parts[0].dtype),
        grid_spec=pltpu.PrefetchScalarGridSpec(
            num_scalar_prefetch=1,
            grid=(1,),
            in_specs=[hbm] * PARTS,
            out_specs=hbm,
            scratch_shapes=[pltpu.SemaphoreType.DMA((PARTS,))],
        ),
        cost_estimate=pl.CostEstimate(flops=0, bytes_accessed=4_000_000, transcendentals=0),
        name="placed",
    )(at, *parts)


def weights_kernel(widths, at_ref, mine_ref, other_ref, *refs):
    outs, sems = refs[:-1], refs[-1]
    y, z, core = at_ref[0], at_ref[1], at_ref[2]
    copies = []
    for q, source in enumerate((mine_ref, other_ref)):
        for r in range(4):
            for s in range(4):
                from_y, from_z = lax.rem(y + 4 - r, 4), lax.rem(z + 4 - s, 4)
                block = ((from_y // 2 * 4 + from_z) * 2 + lax.rem(core + q, 2)) * 2 + lax.rem(from_y, 2)
                n = source.shape[1]
                first = 0
                for k, out in enumerate(outs):
                    window = pl.ds(pl.multiple_of(block * n, n), n)
                    copies.append(pltpu.make_async_copy(
                        source.at[r * 4 + s, :, pl.ds(first, widths[k])],
                        out.at[window, :],
                        sems.at[k, q * 16 + r * 4 + s],
                    ))
                    first += widths[k]
    for copy in copies:
        copy.start()
    for copy in copies:
        copy.wait()


def ordered_weights(at, mine, other, widths):
    model = 2 * mine.shape[0] * mine.shape[1]
    hbm = pl.BlockSpec(memory_space=pl.ANY)
    return pl.pallas_call(
        functools.partial(weights_kernel, widths),
        out_shape=tuple(jax.ShapeDtypeStruct((model, w), mine.dtype) for w in widths),
        grid_spec=pltpu.PrefetchScalarGridSpec(
            num_scalar_prefetch=1,
            grid=(1,),
            in_specs=[hbm] * 2,
            out_specs=(hbm,) * len(widths),
            scratch_shapes=[pltpu.SemaphoreType.DMA((len(widths), 2 * mine.shape[0]))],
        ),
        cost_estimate=pl.CostEstimate(flops=0, bytes_accessed=4_800_000, transcendentals=0),
        name="ordered_weights",
    )(at, mine, other)


def after(value, *others):
    return lax.optimization_barrier((value, *others))[0]


def hops(axis, s):
    n = lax.axis_size(axis)
    return [(i, (i + s) % n) for i in range(n)]


def swapped(blocks, sign):
    return [blocks[0]] + [lax.ppermute(blocks[s], "tp", hops("tp", sign * s)) for s in range(1, PARTS)]


def copied(block):
    return swapped([block] * PARTS, 1)


def from_all(shard, axis):
    return jnp.stack([shard] + [lax.ppermute(shard, axis, hops(axis, s)) for s in range(1, lax.axis_size(axis))])


def summed_on_arrival(whole, axis, peers):
    tiles = whole.reshape(peers, -1, whole.shape[-1])
    return lax.all_to_all(tiles, axis, 0, 0, tiled=True).astype(F32).sum(axis=0)


def in_order(parts, start, axis):
    turned_parts = [parts[-k % PARTS] for k in range(PARTS)]
    size = parts[0].shape[axis]
    both = jnp.concatenate(turned_parts + turned_parts[:-1], axis=axis)
    return lax.dynamic_slice_in_dim(both, (PARTS - start) % PARTS * size, PARTS * size, axis)


def normalized(values):
    centre = values - jnp.mean(values, axis=-1, keepdims=True)
    variance = jnp.mean(centre * centre, axis=-1, keepdims=True)
    inverse = lax.rsqrt(variance + EPSILON)
    return centre * inverse, inverse


def norm_backward(grad_out, normed, inverse, gain_row):
    scaled = grad_out * gain_row
    inner = jnp.mean(scaled, axis=-1, keepdims=True)
    along = jnp.mean(scaled * normed, axis=-1, keepdims=True)
    return inverse * (scaled - inner - normed * along)


def on_device(tokens, cotangent, expert_ids, segment_ids, priority, w_qkv, w_out, norm_gains, norm_shifts,
              qv_bias, w_up, up_bias, w_down, down_bias):
    rows, model = tokens.shape
    channels = w_qkv.shape[2]
    heads = channels // HD
    seq_len = segment_ids.shape[0]
    f_count, c_count = lax.axis_size(FC[:3]), lax.axis_size("ctx")
    groups = f_count * c_count
    ctx_at, tp_at = lax.axis_index("ctx"), lax.axis_index("tp")
    held = w_up.shape[0]
    experts = held * groups
    capacity = (9 * seq_len + 8 * experts - 1) // (8 * experts)
    slots = experts * capacity
    shard = model // groups
    part = rows // PARTS
    width = model // PARTS

    bias_column = jnp.pad(qv_bias.reshape(-1), (0, shard - qv_bias.size))[None]
    small = jnp.concatenate([norm_gains, norm_shifts, bias_column], axis=0).T
    small = jnp.pad(small, ((0, 0), (0, 128 - small.shape[1])))
    pack = jnp.concatenate([jnp.moveaxis(w_qkv, 0, 1).reshape(shard, 3 * channels), w_out.T, small], axis=1)
    plane = from_all(from_all(pack, "z"), Y).reshape(PARTS * PARTS, shard, pack.shape[1])
    chip = jnp.stack([lax.axis_index(Y), lax.axis_index("z"), lax.axis_index("core")])
    qkv_full, out_t, small = ordered_weights(
        chip, plane, lax.ppermute(plane, "core", hops("core", 1)), (3 * channels, channels, 128)
    )
    small = small[:, :6].astype(F32)
    gain_rows = small[:, 0:2].T
    shift_rows = small[:, 2:5].T
    bias_rows = (
        small[:, 5].reshape(groups, shard)[:, : qv_bias.size].reshape(groups, 2, heads, -1)
        .transpose(1, 2, 0, 3).reshape(2, channels)
    )
    out_all = jnp.concatenate(copied(out_t), axis=1)

    owner = expert_ids[:, 0]
    rank = priority[0]
    earlier_ids = lax.ppermute(expert_ids + 1, "ctx", [(0, 1)])[:, 0]
    before = (owner[None, :] == owner[:, None]) & (rank[None, :] < rank[:, None])
    carried = earlier_ids[None, :] == owner[:, None] + 1
    slot = jnp.sum(before.astype(jnp.int32), axis=1) + jnp.sum(carried.astype(jnp.int32), axis=1)
    target = jnp.where(slot < capacity, owner * capacity + slot, slots)
    places = [(tp_at + PARTS - s) % PARTS for s in range(PARTS)]
    target = jnp.concatenate([lax.dynamic_slice_in_dim(target, p * part, part) for p in places])

    def exchanged(sent):
        return lax.all_to_all(sent, FC, 0, 0, tiled=True)

    def sent_rows(columns):
        return to_slots(target, columns, slots).reshape(groups, held * capacity, width)

    cot_columns = [lax.dynamic_slice(cotangent, (p * part, tp_at * width), (part, width)) for p in places]
    cot_sent = sent_rows(jnp.concatenate(cot_columns))

    seg_own = lax.dynamic_slice_in_dim(segment_ids, ctx_at * rows, rows)
    start = jnp.sum((segment_ids[None, :] < seg_own[:, None]).astype(jnp.int32), axis=1)
    start = start + jnp.where(ctx_at == 0, rows, 0)
    at = jnp.concatenate([start[::SIDE] // SIDE, tp_at[None]]).astype(jnp.int32)
    start = start[None, :]
    inputs = tokens.astype(F32)
    normed_all, _ = normalized(inputs)
    first_low = (normed_all * gain_rows[0] + shift_rows[0]).astype(BF)
    k_low = dot(first_low, qkv_full[:, channels : 2 * channels], 1, 0).astype(BF)
    v_low = (dot(first_low, qkv_full[:, 2 * channels :], 1, 0) + bias_rows[1]).astype(BF)
    kv_near = jnp.concatenate([k_low[rows - REACH :], v_low[rows - REACH :]], axis=1)
    kv_far = lax.ppermute(kv_near, "ctx", [(0, 1)])
    cot_got = exchanged(after(cot_sent, kv_near))
    kv_far = jnp.pad(kv_far, ((rows - REACH, 0), (0, 0)))
    k_far, v_far = kv_far[:, :channels], kv_far[:, channels:]
    q_t = (dot(qkv_full[:, :channels], first_low, 0, 1) + bias_rows[0][:, None]).astype(BF)
    mixed_t, exact_t, lse = attend_forward(
        at, q_t, start, jnp.concatenate([k_far, k_low]), jnp.concatenate([v_far, v_low])
    )
    mixed = jnp.concatenate(swapped(jnp.split(mixed_t, PARTS, axis=1), 1))

    inputs_part = lax.dynamic_slice_in_dim(tokens, tp_at * part, part).astype(F32)
    cot_part = lax.dynamic_slice_in_dim(cotangent, tp_at * part, part).astype(F32)
    middle = inputs_part + (dot(mixed, out_all, 0, 1) + shift_rows[2])
    normed_two, inverse_two = normalized(middle)
    second_low = (normed_two * gain_rows[1] + shift_rows[1]).astype(BF)

    def columns_for(values):
        return [
            lax.dynamic_slice_in_dim(values, (tp_at + s) % PARTS * width, width, 1) for s in range(PARTS)
        ]

    second_columns = jnp.concatenate(swapped(columns_for(second_low), 1))
    second_sent = sent_rows(second_columns)
    middle_columns = jnp.concatenate(swapped(columns_for(after(middle.astype(BF), second_sent)), 1))

    cot_mine = join(cot_got, held)
    second_sent, cot_mine = lax.optimization_barrier((second_sent, cot_mine))
    second_got = exchanged(second_sent)
    cot_parts = copied(cot_mine)
    cot_parts = lax.optimization_barrier((*cot_parts, second_got))
    second_got, cot_parts = cot_parts[PARTS], cot_parts[:PARTS]
    mine = join(second_got, held)
    expert_grads = in_order(cot_parts, tp_at, 2)
    active_grad = jnp.einsum("emd,efd->emf", expert_grads, w_down, preferred_element_type=F32)
    parts = [copied(mine[e]) for e in range(held)]
    done = []
    for e in range(held):
        done.append(run_expert(e, at, parts[e], w_up, up_bias, active_grad[e]))
    back_parts = [swapped([o[s] for s in range(PARTS)], -1) for _, _, o in done]
    active_low = jnp.stack([a for a, _, _ in done])
    hidden_grad = jnp.stack([h for _, h, _ in done])
    expert_rows = jnp.stack([in_order(p, tp_at, 1) for p in parts])
    result_part = jnp.einsum("emf,efd->emd", active_low, w_down, preferred_element_type=F32).astype(BF)
    w_down_grad = jnp.einsum("emf,emd->efd", active_low, expert_grads, preferred_element_type=F32)
    w_up_grad = jnp.einsum("emd,emf->edf", expert_rows, hidden_grad, preferred_element_type=F32)
    up_bias_grad = jnp.sum(hidden_grad.astype(F32), axis=1)
    down_bias_grad = jnp.sum(expert_grads.astype(F32), axis=1)

    no_bias = jnp.zeros((held, width), F32)
    back_sent = spread(back_parts, no_bias, capacity)
    back_sent, result_part = lax.optimization_barrier((back_sent, result_part))
    back_got = exchanged(back_sent)
    result_columns = [
        lax.dynamic_slice_in_dim(result_part, (tp_at + PARTS - s) % PARTS * width, width, 2) for s in range(PARTS)
    ]
    result_parts = swapped(result_columns, -1)
    bias_columns = lax.dynamic_slice_in_dim(down_bias, tp_at * width, width, 1).astype(F32)
    result_sent = spread([[p[e] for p in result_parts] for e in range(held)], bias_columns, capacity)
    back_got, w_down_grad, w_up_grad = lax.optimization_barrier((back_got, w_down_grad, w_up_grad))
    grad_columns = to_tokens(target, back_got.reshape(slots, width))
    result_got = exchanged(after(result_sent, grad_columns))
    grad_blocks = swapped(jnp.split(grad_columns, PARTS), -1)
    second_grad = in_order([grad_blocks[-s % PARTS] for s in range(PARTS)], tp_at, 1).astype(F32)

    middle_grad = cot_part + norm_backward(second_grad, normed_two, inverse_two, gain_rows[1])
    branch_low = middle_grad.astype(BF)
    grad_rows_t = dot(out_all, branch_low, 0, 1).astype(BF)
    grad_t = jnp.concatenate(swapped(jnp.split(grad_rows_t, PARTS), -1), axis=1)

    dq_far, dk_far, dv_far = attend_backward(False, at, q_t, grad_t, exact_t, lse, start, k_far, v_far)
    kv_back = lax.ppermute(
        jnp.concatenate([dk_far[rows - REACH :], dv_far[rows - REACH :]], axis=1), "ctx", [(1, 0)]
    )
    dq, dk, dv = attend_backward(True, at, q_t, grad_t, exact_t, lse, start, k_low, v_low, dq_far)

    block_rel = (middle_columns.astype(F32) + to_tokens(target, result_got.reshape(slots, width)).astype(F32)).astype(BF)
    block_columns = in_order(jnp.split(block_rel, PARTS), tp_at, 0)
    block_out = placed(at, copied(block_columns), 1, -1)

    kv_grad = jnp.concatenate([dk, dv], axis=1).astype(F32) + jnp.pad(kv_back, ((rows - REACH, 0), (0, 0))).astype(F32)
    stacked = jnp.concatenate([dq, kv_grad.astype(BF)], axis=1)
    stacked, block_out = lax.optimization_barrier((stacked, block_out))
    first_part = dot(stacked, qkv_full, 1, 1).astype(BF)
    first_blocks = swapped(
        [lax.dynamic_slice_in_dim(first_part, (tp_at + s) % PARTS * part, part) for s in range(PARTS)], 1
    )
    first_grad = sum(b.astype(F32) for b in first_blocks)
    qkv_grad = dot(first_low, after(stacked, first_part), 0, 0).astype(BF)
    qkv_shard = jnp.moveaxis(summed_on_arrival(qkv_grad, FC, groups).reshape(shard, 3, channels), 1, 0)

    out_grad = dot(branch_low, mixed, 0, 1).astype(BF)
    out_sum = summed_on_arrival(after(out_grad, result_got), FC, groups).astype(BF)
    out_blocks = swapped(jnp.split(out_sum, PARTS, axis=1), -1)
    out_shard = sum(b.astype(F32) for b in out_blocks).T

    normed_one, inverse_one = normalized(inputs_part)
    tokens_part = (middle_grad + norm_backward(first_grad, normed_one, inverse_one, gain_rows[0])).astype(BF)
    tokens_grad = placed(at, copied(tokens_part), 0, -1)

    sums = jnp.stack([
        jnp.sum(first_grad * normed_one, axis=0),
        jnp.sum(second_grad * normed_two, axis=0),
        jnp.sum(first_grad, axis=0),
        jnp.sum(second_grad, axis=0),
        jnp.sum(branch_low.astype(F32), axis=0),
    ])
    stacked_sum = jnp.sum(stacked.astype(F32), axis=0)
    bias_sum = jnp.stack([stacked_sum[:channels], stacked_sum[2 * channels :]])
    bias_tiles = bias_sum.reshape(2, heads, groups, -1).transpose(2, 0, 1, 3).reshape(groups, -1)
    sum_tiles = sums.reshape(-1, groups, shard).transpose(1, 0, 2).reshape(groups, -1)
    tail = jnp.concatenate([sum_tiles, bias_tiles], axis=1)
    tail = jnp.pad(tail, ((0, 0), (0, 256 - tail.shape[1]))).reshape(groups, 1, 256)
    tail = jnp.sum(exchanged(tail), axis=0)[0]
    bias_shard = tail[5 * shard : 5 * shard + qv_bias.size].reshape(qv_bias.shape)
    norm_shard = sum(copied(tail[: 5 * shard].reshape(5, shard)))
    return (block_out, tokens_grad, qkv_shard, out_shard, norm_shard[:2], norm_shard[2:], bias_shard,
            w_up_grad, up_bias_grad, w_down_grad, down_bias_grad)


def solution(mesh):
    devices = mesh.devices.reshape(2, 4, 2, mesh.shape["ctx"], mesh.shape["tp"])
    chips = Mesh(devices, ("y_hi", "z", "core", "ctx", "tp"))
    token, weight = P(FC, None), P(None, FC)
    experts = P(FC, None, "tp"), P(FC, "tp"), P(FC, "tp", None), P(FC, None)
    shared = P(None, FC, "tp"), P("tp", FC), weight, weight, P(None, "tp", FC)
    return jax.shard_map(
        on_device,
        mesh=chips,
        in_specs=(token, token, token, P(FC[:3]), token, *shared, *experts),
        out_specs=(token, token, *shared, *experts),
        check_vma=False,
    )
```

time: 586 us -> 689 us (1.18)
  Pallas kernels: 16.9 us -> 257 us
  blocking collectives: 74.8 us -> 0 us
  matrix products: 84.6 us -> 35.5 us
  starting transfers between devices: 82.8 us -> 131 us
  waiting for transfers between devices: 208 us -> 163 us
  between operations: 15.1 us -> 2.82 us
  local copies, waits for them, and re-layouts: 61.3 us -> 49.6 us
  other arithmetic: 31.8 us -> 38.9 us
    pallas_call x0 -> x13, Pallas kernels: none -> 240 us  [the longest x2 131 us: placed(): pl.pallas_call(functools.partial(place_kernel, axis, step), out_shape=jax...]
    ppermute x2 -> x60, waiting for transfers between devices: 12.7 us -> 133 us  [the longest x51 123 us: swapped(): lax.ppermute(blocks[s], 'tp', hops('tp', sign * s))]
    ppermute x2 -> x60, starting transfers between devices: 10.3 us -> 87.8 us  [the longest x51 66.5 us: swapped(): lax.ppermute(blocks[s], 'tp', hops('tp', sign * s))]
    all_to_all x3 -> x0, blocking collectives: 62.8 us -> none  [the longest x2 51.3 us: to_experts(): lax.all_to_all(sent, FC, 0, 0, tiled=True)]
    all_to_all x9 -> x5, waiting for transfers between devices: 71.7 us -> 9.05 us  [exchanged(): return lax.all_to_all(sent, FC, 0, 0, tiled=True)]
    all_gather x6 -> x0, waiting for transfers between devices: 62.3 us -> none  [the longest x2 30.2 us: to_experts(): return lax.all_gather(mine, 'tp', axis=2, tiled=True)]
    reduce_scatter x3 -> x0, waiting for transfers between devices: 52.1 us -> none  [the longest x1 25 us: on_device(): lax.psum_scatter(input_part, 'tp', scatter_dimension=2, tiled=True)]
    dot_general x12 -> x8, matrix products: 38.8 us -> 16.7 us  [dot(): lax.dot_general(a, b, (((ca,), (cb,)), ((), ())), preferred_element_type=...]
  transfers between devices with their start and end apart: 23 -> 68, of which waited for: 17 -> 32; matrix products, arithmetic and copies ran while one was open for 22% -> 14% of each run, Pallas kernels for 3% -> 16%
where the time goes in v2:
time: 689 us; the launch traced here: 679 us
  Pallas kernels  257 us (37%)
  waiting for transfers between devices  163 us (24%)
  starting transfers between devices  131 us (19%)
  local copies, waits for them, and re-layouts  49.6 us (7%)
  other arithmetic  38.9 us (6%)
  matrix products  35.5 us (5%)
    pallas_call x2, Pallas kernels, placed(): pl.pallas_call(functools.partial(place_kernel, axis, step), out_shape=jax...  131 us
    ppermute x51, waiting for transfers between devices, swapped(): lax.ppermute(blocks[s], 'tp', hops('tp', sign * s))  123 us
    pallas_call x1, Pallas kernels, ordered_weights(): pl.pallas_call(functools.partial(weights_kernel, widths), out_shape=tuple...  74.1 us
    ppermute x51, starting transfers between devices, swapped(): lax.ppermute(blocks[s], 'tp', hops('tp', sign * s))  66.5 us
    all_to_all x5, starting transfers between devices, exchanged(): return lax.all_to_all(sent, FC, 0, 0, tiled=True)  33.3 us
    unnamed x159, local copies, waits for them, and re-layouts  20.8 us
    all_to_all x2, waiting for transfers between devices, summed_on_arrival(): return lax.all_to_all(tiles, axis, 0, 0, tiled=True).astype(F32).sum(axis=0)  20.7 us
    pallas_call x2, Pallas kernels, run_expert(): pl.pallas_call(expert_kernel, out_shape=(jax.ShapeDtypeStruct((rows, inne...  20.1 us
  transfers between devices with their start and end apart: 68, of which 32 were waited for; matrix products, arithmetic and copies ran while one was open for 14% of the time, Pallas kernels for 16%

profile of v2, /device:TPU:0, one launch (start us, length us, event | category | flops | bytes accessed | tf_op | source)
XLA Modules:
  0.0 678.5 jit_solution(9723593913688418865)
XLA Ops:
  27.4 5.3 collective-permute-done.4
  41.0 74.1 %ordered_weights.1 = (bf16[1024,768]{1,0:T(8,128)(2,1)}, bf16[1024,256]{1,0:T(8,128)(2,1)}, bf16[1024,128]{1,0:T(8,128)(2,1)}) custom-call(s32[3]{0:T(128)} %pad_add_fusion.2.at_ref, bf16[16,32,1152]{2,1,0:T(8,128)(2,1)} %bitcast.16.mine_ref, bf16[16,32,1152]{2,1,0:T(8,128)(2,1)} %collective-permute-done.6.other_ref), custom_call_target="tpu_custom_call" | custom-call | bytes 4800000 | tf_op jit(solution)/shard_map/ordered_weights/pallas_call | solution.py:432
  147.9 6.5 attend_forward.1
  182.5 7.1 %all-to-all-start.1 = ((bf16[32,72,256]{2,1,0:T(8,128)(2,1)}), bf16[32,72,256]{2,1,0:T(8,128)(2,1)S(1)}, u32[]{:S(2)}, u32[]{:S(2)}) async-start(bf16[32,72,256]{2,1,0:T(8,128)(2,1)} %bitcast.129), calls=%async_computation.1 | async-start | bytes 2359296 | tf_op jit(solution)/shard_map/all_to_all | solution.py:540
  197.4 9.1 %collective-permute-done.20 = bf16[2,576,256]{2,1,0:T(8,128)(2,1)} collective-permute-done((bf16[2,576,256]{2,1,0:T(8,128)(2,1)S(1)}, bf16[2,576,256]{2,1,0:T(8,128)(2,1)}, u32[]{:S(2)}, u32[]{:S(2)}) %collective-permute-start.20) | collective-permute-done | bytes 589856 | tf_op jit(solution)/shard_map/ppermute | solution.py:457
  209.2 11.6 %collective-permute-done.18 = bf16[2,576,256]{2,1,0:T(8,128)(2,1)} collective-permute-done((bf16[2,576,256]{2,1,0:T(8,128)(2,1)S(1)}, bf16[2,576,256]{2,1,0:T(8,128)(2,1)}, u32[]{:S(2)}, u32[]{:S(2)}) %collective-permute-start.18) | collective-permute-done | bytes 589856 | tf_op jit(solution)/shard_map/ppermute | solution.py:457
  239.5 10.0 %expert.3 = (bf16[576,1024]{1,0:T(8,128)(2,1)S(1)}, bf16[576,1024]{1,0:T(8,128)(2,1)S(1)}, bf16[4,576,256]{2,1,0:T(8,128)(2,1)S(1)}) custom-call(s32[5]{0:T(128)S(1)} %pad_add_fusion.1.at_ref.refs_0_, bf16[576,256]{1,0:T(8,128)(2,1)S(1)} %get-tuple-element.191.r0, bf16[576,256]{1,0:T(8,128)(2,1)S(1)} %collective-permute-done.27.r1, ...), custom_call_target="tpu_custom_call" | custom-call | flops 2400000000 | bytes 8000000 | tf_op jit(solution)/shard_map/expert/pallas_call | solution.py:346
  250.7 10.1 %expert.2 = (bf16[576,1024]{1,0:T(8,128)(2,1)S(1)}, bf16[576,1024]{1,0:T(8,128)(2,1)S(1)}, bf16[4,576,256]{2,1,0:T(8,128)(2,1)S(1)}) custom-call(s32[5]{0:T(128)S(1)} %pad_add_fusion.1.at_ref.refs_0_, bf16[576,256]{1,0:T(8,128)(2,1)S(1)} %get-tuple-element.192.r0, bf16[576,256]{1,0:T(8,128)(2,1)S(1)} %collective-permute-done.21.r1, ...), custom_call_target="tpu_custom_call" | custom-call | flops 2400000000 | bytes 8000000 | tf_op jit(solution)/shard_map/expert/pallas_call | solution.py:346
  278.9 5.9 fusion.10
  284.8 5.2 collective-permute-done.32.refs_7_
  292.4 7.4 %all-to-all-start.2 = ((bf16[32,72,256]{2,1,0:T(8,128)(2,1)}), bf16[32,72,256]{2,1,0:T(8,128)(2,1)}, u32[]{:S(2)}, u32[]{:S(2)}) async-start(bf16[32,72,256]{2,1,0:T(8,128)(2,1)} %spread.2), calls=%async_computation.2 | async-start | bytes 2359296 | tf_op jit(solution)/shard_map/all_to_all | solution.py:540
  305.0 6.3 fusion.6
  326.1 8.0 %collective-permute-done.44 = bf16[2,576,256]{2,1,0:T(8,128)(2,1)} collective-permute-done((bf16[2,576,256]{2,1,0:T(8,128)(2,1)}, bf16[2,576,256]{2,1,0:T(8,128)(2,1)}, u32[]{:S(2)}, u32[]{:S(2)}) %collective-permute-start.44) | collective-permute-done | bytes 589856 | tf_op jit(solution)/shard_map/ppermute | solution.py:457
  335.3 11.5 %collective-permute-done.33 = bf16[256,256]{1,0:T(8,128)(2,1)S(1)} collective-permute-done((bf16[256,256]{1,0:T(8,128)(2,1)S(1)}, bf16[256,256]{1,0:T(8,128)(2,1)S(1)}, u32[]{:S(2)}, u32[]{:S(2)}) %collective-permute-start.33) | collective-permute-done | bytes 131104 | tf_op jit(solution)/shard_map/ppermute | solution.py:457
  358.9 7.3 %all-to-all-start.3 = ((bf16[32,72,256]{2,1,0:T(8,128)(2,1)}), bf16[32,72,256]{2,1,0:T(8,128)(2,1)S(1)}, u32[]{:S(2)}, u32[]{:S(2)}) async-start(bf16[32,72,256]{2,1,0:T(8,128)(2,1)} %spread.3), calls=%async_computation.3 | async-start | bytes 2359296 | tf_op jit(solution)/shard_map/all_to_all | solution.py:540
  392.6 9.0 %attend_near.1 = (bf16[1024,256]{1,0:T(8,128)(2,1)S(1)}, bf16[1024,256]{1,0:T(8,128)(2,1)S(1)}, bf16[1024,256]{1,0:T(8,128)(2,1)S(1)}) custom-call(s32[5]{0:T(128)S(1)} %pad_add_fusion.1.at_ref.refs_0_, bf16[256,1024]{1,0:T(8,128)(2,1)S(1)} %copy-done.18, bf16[256,1024]{1,0:T(8,128)(2,1)S(1)} %copy-done.13, f32[256,1024]{1,0:T(8,128)S(1)} %copy-done.21, ...), custom_call_target="tpu_custom_call" | custom-call | flops 8999999488 | bytes 6000000 | tf_op jit(solution)/shard_map/attend_near/pallas_call | solution.py:198
  405.4 9.6 %collective-permute-done.46.refs_1_ = bf16[1024,256]{1,0:T(8,128)(2,1)} collective-permute-done((bf16[1024,256]{1,0:T(8,128)(2,1)S(1)}, bf16[1024,256]{1,0:T(8,128)(2,1)}, u32[]{:S(2)}, u32[]{:S(2)}) %collective-permute-start.46) | collective-permute-done | bytes 524320 | tf_op jit(solution)/shard_map/ppermute | solution.py:457
  415.0 65.3 %placed.2 = bf16[1024,1024]{1,0:T(8,128)(2,1)} custom-call(s32[5]{0:T(128)} %copy-done.14, bf16[1024,256]{1,0:T(8,128)(2,1)} %copy-done.34, bf16[1024,256]{1,0:T(8,128)(2,1)} %collective-permute-done.46.refs_1_, bf16[1024,256]{1,0:T(8,128)(2,1)} %copy-done.40, bf16[1024,256]{1,0:T(8,128)(2,1)} %copy-done.39), custom_call_target="tpu_custom_call" | custom-call | bytes 4000000 | tf_op jit(solution)/shard_map/placed/pallas_call | solution.py:389
  488.7 21.5 %collective-permute-done.49 = bf16[256,1024]{1,0:T(8,128)(2,1)} collective-permute-done((bf16[256,1024]{1,0:T(8,128)(2,1)S(1)}, bf16[256,1024]{1,0:T(8,128)(2,1)}, u32[]{:S(2)}, u32[]{:S(2)}) %collective-permute-start.49) | collective-permute-done | bytes 524320 | tf_op jit(solution)/shard_map/ppermute | solution.py:457
  515.2 7.6 %all-to-all-start.6 = ((f32[32,1,256]{2,1,0:T(1,128)}), f32[32,1,256]{2,1,0:T(1,128)S(1)}, u32[]{:S(2)}, u32[]{:S(2)}) async-start(f32[32,1,256]{2,1,0:T(1,128)} %reshape.188), calls=%async_computation.6 | async-start | bytes 65536 | tf_op jit(solution)/shard_map/all_to_all | solution.py:540
  525.0 5.4 all-to-all-done.6
  541.8 20.7 %all-to-all-done.5 = bf16[32,32,1024]{2,1,0:T(8,128)(2,1)S(1)} async-done(((bf16[32,32,1024]{2,1,0:T(8,128)(2,1)}), bf16[32,32,1024]{2,1,0:T(8,128)(2,1)S(1)}, u32[]{:S(2)}, u32[]{:S(2)}) %all-to-all-start.5) | async-done | bytes 2097184 | tf_op jit(solution)/shard_map/all_to_all | solution.py:470
  581.2 16.5 %collective-permute-done.60 = f32[5,32]{1,0:T(8,128)S(1)} collective-permute-done((f32[5,32]{1,0:T(8,128)S(1)}, f32[5,32]{1,0:T(8,128)S(1)}, u32[]{:S(2)}, u32[]{:S(2)}) %collective-permute-start.60) | collective-permute-done | bytes 672 | tf_op jit(solution)/shard_map/ppermute | solution.py:457
  604.2 65.5 %placed.3 = bf16[1024,1024]{1,0:T(8,128)(2,1)} custom-call(s32[5]{0:T(128)} %copy-done.14, bf16[256,1024]{1,0:T(8,128)(2,1)} %fusion.28.refs_0_, bf16[256,1024]{1,0:T(8,128)(2,1)} %collective-permute-done.52.refs_1_, bf16[256,1024]{1,0:T(8,128)(2,1)} %collective-permute-done.53.refs_2_, bf16[256,1024]{1,0:T(8,128)(2,1)} %collective-permute-done.54.refs_3_), custom_call_target="tpu_custom_call" | custom-call | bytes 4000000 | tf_op jit(solution)/shard_map/placed/pallas_call | solution.py:389
  (431 shorter events, 269.1 us)
Async XLA Ops:
  11.8 28.4 %collective-permute-start.14 = (s32[1024,1]{0,1:T(1,128)S(1)}, s32[1024,1]{0,1:T(1,128)S(1)}, u32[]{:S(2)}, u32[]{:S(2)}) collective-permute-start(s32[1024,1]{0,1:T(1,128)S(1)} %broadcast_add_fusion), channel_id=1, source_target_pairs={{0,4},{1,5},{2,6},{3,7},{8,12},{9,13},{10,14},{11,15},{16,20},{17,... | collective-permute-start | bytes 12296 | tf_op jit(solution)/shard_map/ppermute | solution.py:531
  134.0 26.1 %collective-permute-start.9 = (bf16[1024,256]{1,0:T(8,128)(2,1)}, bf16[1024,256]{1,0:T(8,128)(2,1)}, u32[]{:S(2)}, u32[]{:S(2)}) collective-permute-start(bf16[1024,256]{1,0:T(8,128)(2,1)} %get-tuple-element.50), channel_id=1, source_target_pairs={{0,3},{1,0},{2,1},{3,2},{4,7},{5,4},{6,5},{7,6},{8,11},{9,8},{10,9... | collective-permute-start | bytes 1572872 | tf_op jit(solution)/shard_map/ppermute | solution.py:457
  135.8 23.2 %collective-permute-start.8 = (bf16[1024,256]{1,0:T(8,128)(2,1)}, bf16[1024,256]{1,0:T(8,128)(2,1)}, u32[]{:S(2)}, u32[]{:S(2)}) collective-permute-start(bf16[1024,256]{1,0:T(8,128)(2,1)} %get-tuple-element.50), channel_id=1, source_target_pairs={{0,2},{1,3},{2,0},{3,1},{4,6},{5,7},{6,4},{7,5},{8,10},{9,11},{10,... | collective-permute-start | bytes 1572872 | tf_op jit(solution)/shard_map/ppermute | solution.py:457
  138.0 44.2 %all-to-all-start = ((bf16[32,72,256]{2,1,0:T(8,128)(2,1)}), bf16[32,72,256]{2,1,0:T(8,128)(2,1)S(1)}, u32[]{:S(2)}, u32[]{:S(2)}) async-start(bf16[32,72,256]{2,1,0:T(8,128)(2,1)} %bitcast.128), calls=%async_computation | async-start | bytes 2359296 | tf_op jit(solution)/shard_map/all_to_all | solution.py:540
  182.5 38.4 %all-to-all-start.1 = ((bf16[32,72,256]{2,1,0:T(8,128)(2,1)}), bf16[32,72,256]{2,1,0:T(8,128)(2,1)S(1)}, u32[]{:S(2)}, u32[]{:S(2)}) async-start(bf16[32,72,256]{2,1,0:T(8,128)(2,1)} %bitcast.129), calls=%async_computation.1 | async-start | bytes 2359296 | tf_op jit(solution)/shard_map/all_to_all | solution.py:540
  192.4 28.4 %collective-permute-start.18 = (bf16[2,576,256]{2,1,0:T(8,128)(2,1)S(1)}, bf16[2,576,256]{2,1,0:T(8,128)(2,1)}, u32[]{:S(2)}, u32[]{:S(2)}) collective-permute-start(bf16[2,576,256]{2,1,0:T(8,128)(2,1)S(1)} %join.2), channel_id=1, source_target_pairs={{0,1},{1,2},{2,3},{3,0},{4,5},{5,6},{6,7},{7,4},{8,9},{9,10},{10,1... | collective-permute-start | bytes 1769480 | tf_op jit(solution)/shard_map/ppermute | solution.py:457
  223.6 26.0 %collective-permute-start.23 = (bf16[576,256]{1,0:T(8,128)(2,1)S(1)}, bf16[576,256]{1,0:T(8,128)(2,1)S(1)}, u32[]{:S(2)}, u32[]{:S(2)}) collective-permute-start(bf16[576,256]{1,0:T(8,128)(2,1)S(1)} %get-tuple-element.192.r0), channel_id=1, source_target_pairs={{0,3},{1,0},{2,1},{3,2},{4,7},{5,4},{6,5},{7,6},{8,11},{9,8},{10,9... | collective-permute-start | bytes 884744 | tf_op jit(solution)/shard_map/ppermute | solution.py:457
  226.0 23.6 %collective-permute-start.22 = (bf16[576,256]{1,0:T(8,128)(2,1)S(1)}, bf16[576,256]{1,0:T(8,128)(2,1)S(1)}, u32[]{:S(2)}, u32[]{:S(2)}) collective-permute-start(bf16[576,256]{1,0:T(8,128)(2,1)S(1)} %get-tuple-element.192.r0), channel_id=1, source_target_pairs={{0,2},{1,3},{2,0},{3,1},{4,6},{5,7},{6,4},{7,5},{8,10},{9,11},{10,... | collective-permute-start | bytes 884744 | tf_op jit(solution)/shard_map/ppermute | solution.py:457
  261.0 23.9 %collective-permute-start.25 = (bf16[576,256]{1,0:T(8,128)(2,1)S(1)}, bf16[576,256]{1,0:T(8,128)(2,1)S(1)}, u32[]{:S(2)}, u32[]{:S(2)}) collective-permute-start(bf16[576,256]{1,0:T(8,128)(2,1)S(1)} %get-tuple-element.175), channel_id=1, source_target_pairs={{0,2},{1,3},{2,0},{3,1},{4,6},{5,7},{6,4},{7,5},{8,10},{9,11},{10,... | collective-permute-start | bytes 884744 | tf_op jit(solution)/shard_map/ppermute | solution.py:457
  264.6 25.4 %collective-permute-start.32 = (bf16[576,256]{1,0:T(8,128)(2,1)S(1)}, bf16[576,256]{1,0:T(8,128)(2,1)S(1)}, u32[]{:S(2)}, u32[]{:S(2)}) collective-permute-start(bf16[576,256]{1,0:T(8,128)(2,1)S(1)} %get-tuple-element.170), channel_id=1, source_target_pairs={{0,1},{1,2},{2,3},{3,0},{4,5},{5,6},{6,7},{7,4},{8,9},{9,10},{10,1... | collective-permute-start | bytes 884744 | tf_op jit(solution)/shard_map/ppermute | solution.py:457
  265.5 24.5 %collective-permute-start.31 = (bf16[576,256]{1,0:T(8,128)(2,1)S(1)}, bf16[576,256]{1,0:T(8,128)(2,1)S(1)}, u32[]{:S(2)}, u32[]{:S(2)}) collective-permute-start(bf16[576,256]{1,0:T(8,128)(2,1)S(1)} %get-tuple-element.171), channel_id=1, source_target_pairs={{0,2},{1,3},{2,0},{3,1},{4,6},{5,7},{6,4},{7,5},{8,10},{9,11},{10,... | collective-permute-start | bytes 884744 | tf_op jit(solution)/shard_map/ppermute | solution.py:457
  292.4 27.7 %all-to-all-start.2 = ((bf16[32,72,256]{2,1,0:T(8,128)(2,1)}), bf16[32,72,256]{2,1,0:T(8,128)(2,1)}, u32[]{:S(2)}, u32[]{:S(2)}) async-start(bf16[32,72,256]{2,1,0:T(8,128)(2,1)} %spread.2), calls=%async_computation.2 | async-start | bytes 2359296 | tf_op jit(solution)/shard_map/all_to_all | solution.py:540
  311.4 22.7 %collective-permute-start.44 = (bf16[2,576,256]{2,1,0:T(8,128)(2,1)}, bf16[2,576,256]{2,1,0:T(8,128)(2,1)}, u32[]{:S(2)}, u32[]{:S(2)}) collective-permute-start(bf16[2,576,256]{2,1,0:T(8,128)(2,1)} %get-tuple-element.161), channel_id=1, source_target_pairs={{0,2},{1,3},{2,0},{3,1},{4,6},{5,7},{6,4},{7,5},{8,10},{9,11},{10,... | collective-permute-start | bytes 1769480 | tf_op jit(solution)/shard_map/ppermute | solution.py:457
  314.9 41.2 %collective-permute-start.43 = (bf16[2,576,256]{2,1,0:T(8,128)(2,1)}, bf16[2,576,256]{2,1,0:T(8,128)(2,1)}, u32[]{:S(2)}, u32[]{:S(2)}) collective-permute-start(bf16[2,576,256]{2,1,0:T(8,128)(2,1)} %get-tuple-element.162), channel_id=1, source_target_pairs={{0,3},{1,0},{2,1},{3,2},{4,7},{5,4},{6,5},{7,6},{8,11},{9,8},{10,9... | collective-permute-start | bytes 1769480 | tf_op jit(solution)/shard_map/ppermute | solution.py:457
  323.6 23.2 %collective-permute-start.34 = (bf16[256,256]{1,0:T(8,128)(2,1)S(1)}, bf16[256,256]{1,0:T(8,128)(2,1)S(1)}, u32[]{:S(2)}, u32[]{:S(2)}) collective-permute-start(bf16[256,256]{1,0:T(8,128)(2,1)S(1)} %get-tuple-element.203), channel_id=1, source_target_pairs={{0,2},{1,3},{2,0},{3,1},{4,6},{5,7},{6,4},{7,5},{8,10},{9,11},{10,... | collective-permute-start | bytes 393224 | tf_op jit(solution)/shard_map/ppermute | solution.py:457
  358.9 25.7 %all-to-all-start.3 = ((bf16[32,72,256]{2,1,0:T(8,128)(2,1)}), bf16[32,72,256]{2,1,0:T(8,128)(2,1)S(1)}, u32[]{:S(2)}, u32[]{:S(2)}) async-start(bf16[32,72,256]{2,1,0:T(8,128)(2,1)} %spread.3), calls=%async_computation.3 | async-start | bytes 2359296 | tf_op jit(solution)/shard_map/all_to_all | solution.py:540
  483.7 26.5 %collective-permute-start.49 = (bf16[256,1024]{1,0:T(8,128)(2,1)S(1)}, bf16[256,1024]{1,0:T(8,128)(2,1)}, u32[]{:S(2)}, u32[]{:S(2)}) collective-permute-start(bf16[256,1024]{1,0:T(8,128)(2,1)S(1)} %get-tuple-element.163), channel_id=1, source_target_pairs={{0,1},{1,2},{2,3},{3,0},{4,5},{5,6},{6,7},{7,4},{8,9},{9,10},{10,1... | collective-permute-start | bytes 1572872 | tf_op jit(solution)/shard_map/ppermute | solution.py:457
  485.6 24.6 %collective-permute-start.51 = (bf16[256,1024]{1,0:T(8,128)(2,1)S(1)}, bf16[256,1024]{1,0:T(8,128)(2,1)}, u32[]{:S(2)}, u32[]{:S(2)}) collective-permute-start(bf16[256,1024]{1,0:T(8,128)(2,1)S(1)} %get-tuple-element.164), channel_id=1, source_target_pairs={{0,3},{1,0},{2,1},{3,2},{4,7},{5,4},{6,5},{7,6},{8,11},{9,8},{10,9... | collective-permute-start | bytes 1572872 | tf_op jit(solution)/shard_map/ppermute | solution.py:457
  487.1 23.2 %collective-permute-start.50 = (bf16[256,1024]{1,0:T(8,128)(2,1)S(1)}, bf16[256,1024]{1,0:T(8,128)(2,1)}, u32[]{:S(2)}, u32[]{:S(2)}) collective-permute-start(bf16[256,1024]{1,0:T(8,128)(2,1)S(1)} %get-tuple-element.165), channel_id=1, source_target_pairs={{0,2},{1,3},{2,0},{3,1},{4,6},{5,7},{6,4},{7,5},{8,10},{9,11},{10,... | collective-permute-start | bytes 1572872 | tf_op jit(solution)/shard_map/ppermute | solution.py:457
  530.4 32.0 %all-to-all-start.5 = ((bf16[32,32,1024]{2,1,0:T(8,128)(2,1)}), bf16[32,32,1024]{2,1,0:T(8,128)(2,1)S(1)}, u32[]{:S(2)}, u32[]{:S(2)}) async-start(bf16[32,32,1024]{2,1,0:T(8,128)(2,1)} %bitcast.62), calls=%async_computation.5 | async-start | bytes 4194304 | tf_op jit(solution)/shard_map/all_to_all | solution.py:470
  563.7 110.0 %all-to-all-start.4 = ((bf16[32,32,768]{2,1,0:T(8,128)(2,1)}), bf16[32,32,768]{2,1,0:T(8,128)(2,1)}, u32[]{:S(2)}, u32[]{:S(2)}) async-start(bf16[32,32,768]{2,1,0:T(8,128)(2,1)} %bitcast.141), calls=%async_computation.4 | async-start | bytes 3145728 | tf_op jit(solution)/shard_map/all_to_all | solution.py:470
  571.6 32.6 %collective-permute-start.54 = (bf16[256,1024]{1,0:T(8,128)(2,1)}, bf16[256,1024]{1,0:T(8,128)(2,1)}, u32[]{:S(2)}, u32[]{:S(2)}) collective-permute-start(bf16[256,1024]{1,0:T(8,128)(2,1)} %fusion.28.refs_0_), channel_id=1, source_target_pairs={{0,3},{1,0},{2,1},{3,2},{4,7},{5,4},{6,5},{7,6},{8,11},{9,8},{10,9... | collective-permute-start | bytes 1572872 | tf_op jit(solution)/shard_map/ppermute | solution.py:457
  574.5 29.7 %collective-permute-start.53 = (bf16[256,1024]{1,0:T(8,128)(2,1)}, bf16[256,1024]{1,0:T(8,128)(2,1)}, u32[]{:S(2)}, u32[]{:S(2)}) collective-permute-start(bf16[256,1024]{1,0:T(8,128)(2,1)} %fusion.28.refs_0_), channel_id=1, source_target_pairs={{0,2},{1,3},{2,0},{3,1},{4,6},{5,7},{6,4},{7,5},{8,10},{9,11},{10,... | collective-permute-start | bytes 1572872 | tf_op jit(solution)/shard_map/ppermute | solution.py:457
  574.5 29.7 %collective-permute-start.52 = (bf16[256,1024]{1,0:T(8,128)(2,1)}, bf16[256,1024]{1,0:T(8,128)(2,1)}, u32[]{:S(2)}, u32[]{:S(2)}) collective-permute-start(bf16[256,1024]{1,0:T(8,128)(2,1)} %fusion.28.refs_0_), channel_id=1, source_target_pairs={{0,1},{1,2},{2,3},{3,0},{4,5},{5,6},{6,7},{7,4},{8,9},{9,10},{10,1... | collective-permute-start | bytes 1572872 | tf_op jit(solution)/shard_map/ppermute | solution.py:457
  (105 other events, 1855.9 us)
